TPU v7x, 32 devices: a whole 2x2x4 slice. The times are simulated.
32 devices in a mesh: row: 16 (over z, y, x), col: 2 (over core).
Axes of the slice: x: 2, y: 2, z: 4, core: 2. Of those that a mesh axis runs over, the one named last changes fastest.
Arguments:
- tiles: float32 [16, 2, 64, 128, 128], P('row', 'col'), may hold values from -0.125 to 0.125
- tile_rows: int32 [16, 2, 64], P('row', 'col'), may hold values from 0 to 15, as said below
- tile_cols: int32 [16, 2, 64], P('row', 'col'), may hold values from 0 to 63, as said below
- exponents: int32 [16384], P('col'), may hold values from 0 to 3
- u_basis: float32 [64, 32768], P(None, 'row'), may hold values from -6 to 6
- v_basis: float32 [64, 16384], P(None, ('col', 'row')), may hold values from -6 to 6
- prior: float32 [64, 64], replicated, may hold values from -0.75 to 0.75
Outputs:
- u_next: float32 [64, 32768], P(None, ('row', 'col'))
- v_next: float32 [64, 16384], P(None, ('col', 'row'))
- v_factor: float32 [64, 64], replicated
- u_factor: float32 [64, 64], replicated
Inputs may be any that keep to these rules, and one draw needn't show every extreme that they name: `tile_rows`: within each grid cell every tile row of 0 to 15 appears exactly 64 / 16 times. `tile_cols`: within each grid cell every tile column of 0 to 63 appears exactly 64 / 64 times.
All inputs are finite; a program needn't handle non-finite values.
Results may differ from a plain program's by a relative error of at most 0.00018.
Values sent between devices are 32-bit elements; how exact they have to be, the bound alone decides.
A program may use at most 64 MiB of HBM per device.

v0:
```python
import math

import jax
import jax.numpy as jnp
from jax import lax
from jax.sharding import PartitionSpec as P

HIGH = lax.Precision.HIGHEST


def lower_solve(factor, rhs):
    return lax.linalg.triangular_solve(factor, rhs, left_side=True, lower=True)


def per_device(tiles, tile_rows, tile_cols, exponents, u_basis, v_basis, prior):
    local_tiles = tiles[0, 0]
    rows_here = tile_rows[0, 0]
    cols_here = tile_cols[0, 0]
    count, tl, _ = local_tiles.shape
    width, block_rows = u_basis.shape
    block_cols = exponents.shape[0]
    rows_tiles = block_rows // tl
    cols_tiles = block_cols // tl
    total_rows = block_rows * lax.axis_size("row")
    total_cols = block_cols * lax.axis_size("col")
    v_piece = v_basis.shape[1]
    u_piece = block_rows // lax.axis_size("col")
    col_scale = jnp.exp2(-exponents.astype(jnp.float32))
    lowtri = jnp.tril(prior)
    col_hits = (cols_here[:, None] == jnp.arange(cols_tiles, dtype=jnp.int32)[None, :]).astype(
        jnp.float32
    )
    row_hits = (rows_here[:, None] == jnp.arange(rows_tiles, dtype=jnp.int32)[None, :]).astype(
        jnp.float32
    )
    picked = jnp.take(u_basis.reshape(width, rows_tiles, tl), rows_here, axis=1)
    prod = jnp.einsum("sta,tab->stb", picked, local_tiles, precision=HIGH)
    partial_value = (
        jnp.einsum("stb,tc->scb", prod, col_hits, precision=HIGH).reshape(width, block_cols)
        * col_scale
    )
    offset = lax.axis_index("row") * v_piece
    own_term = jnp.dot(lowtri, v_basis, precision=HIGH)
    slot = lax.dynamic_slice_in_dim(partial_value, offset, v_piece, 1) - own_term
    partial_value = lax.dynamic_update_slice_in_dim(partial_value, slot, offset, 1)
    pt_piece = lax.psum_scatter(partial_value, "row", scatter_dimension=1, tiled=True)
    gram = lax.psum(jnp.dot(pt_piece, pt_piece.T, precision=HIGH), ("row", "col"))
    v_factor = jnp.linalg.cholesky(gram / total_cols)
    v_next = lower_solve(v_factor, pt_piece)
    source = lax.all_gather(v_next, "row", axis=1, tiled=True)
    factor = math.sqrt(total_rows / total_cols)
    scaled = (source * col_scale).reshape(width, cols_tiles, tl)
    chosen = jnp.take(scaled, cols_here, axis=1)
    products = jnp.einsum("stb,tab->sta", chosen, local_tiles, precision=HIGH)
    terms = factor * jnp.einsum("sta,tr->sra", products, row_hits, precision=HIGH).reshape(
        width, block_rows
    )
    summed = lax.psum_scatter(terms, "col", scatter_dimension=1, tiled=True)
    u_own = lax.dynamic_slice_in_dim(u_basis, lax.axis_index("col") * u_piece, u_piece, 1)
    qt_piece = summed - jnp.dot(v_factor.T, u_own, precision=HIGH)
    ugram = lax.psum(jnp.dot(qt_piece, qt_piece.T, precision=HIGH), ("row", "col"))
    u_factor = jnp.linalg.cholesky(ugram / total_rows)
    u_next = lower_solve(u_factor, qt_piece)
    return (u_next, v_next, v_factor, u_factor)


def solution(mesh):
    placed = (
        P("row", "col", None, None, None),
        P("row", "col", None),
        P("row", "col", None),
        P("col"),
        P(None, "row"),
        P(None, ("col", "row")),
        P(),
    )
    return jax.shard_map(
        per_device,
        mesh=mesh,
        in_specs=placed,
        out_specs=(P(None, ("row", "col")), P(None, ("col", "row")), P(), P()),
        check_vma=False,
    )
```

profile of v0, /device:TPU:0, one launch (start us, length us, event | category | flops | bytes accessed | tf_op | source)
XLA Modules:
  0.0 304.7 jit_solution(10135979052091601112)
XLA Ops:
  7.2 0.0 copy-start
  7.2 0.0 reduce-scatter.3.cloned.1.call-start
  7.2 0.7 fusion.48
  7.9 0.7 compare_and_fusion
  8.6 0.0 copy-done
  8.7 0.8 multiply_exponential_fusion
  9.5 0.7 gather_fusion
  10.2 0.0 copy-start.5
  10.2 5.7 %fusion.12 = f32[64,64,128]{2,0,1:T(8,128)S(1)} fusion(f32[1,1,64,128,128]{4,3,2,1,0:T(8,128)} %param.8, f32[64,64,128]{2,1,0:T(8,128)S(1)} %gather_fusion, pred[64]{0:T(512)(128)(4,1)S(1)} %get-tuple-element.9), kind=kOutput, calls=%fused_computation.17 | convolution fusion | flops 805830656 | bytes 8388672 | tf_op jit(solution)/shard_map/sta,tab->stb/dot_general | solution.py:37
  15.9 0.0 copy-done.5
  15.9 2.5 fusion.8
  18.4 0.0 copy-start.3
  18.4 0.0 copy-start.4
  18.4 1.2 bitcast_multiply_fusion
  19.6 0.0 copy-done.3
  19.6 0.0 copy-done.4
  19.6 0.3 fusion.25
  19.9 0.0 copy-start.1
  19.9 1.3 copy-done.1
  21.3 0.0 reduce-scatter.3.cloned.1.call-update
  21.3 0.0 all-gather.2.cloned.1.call-start
  21.3 83.4 %reduce-scatter.3.cloned.1.call-done = f32[64,512]{1,0:T(8,128)} async-done(((f32[64,8192]{1,0:T(8,128)}), f32[64,512]{1,0:T(8,128)}) %reduce-scatter.3.cloned.1.call-update) | async-done | bytes 131088 | tf_op jit(solution)/shard_map/reduce_scatter | solution.py:46
  104.8 1.2 fusion.53
  106.0 37.0 %psum.14 = f32[64,64]{0,1:T(8,128)S(1)} all-reduce(f32[64,64]{0,1:T(8,128)S(1)} %fusion.53), channel_id=1, replica_groups=mesh['row'=16,'col'=2] {'row','col'}, use_global_device_ids=true, to_apply=%region_1.2 | all-reduce | flops 4096 | bytes 32768 | tf_op jit(solution)/shard_map/psum | solution.py:47
  143.0 0.1 copy.23
  143.1 5.8 %cholesky.44 = f32[64,64]{1,0:T(8,128)S(1)} custom-call(f32[64,64]{1,0:T(8,128)S(1)} %fusion.36), custom_call_target="Cholesky" | custom-call | tf_op jit(solution)/shard_map/jit(cholesky)/cholesky | solution.py:48
  149.0 0.6 compare_reduce_fusion.1
  149.7 0.7 select_bitcast_fusion.1
  150.3 0.0 copy-start.2
  150.3 4.9 %custom-call.8 = f32[1,64,64]{1,2,0:T(8,128)S(1)} custom-call(f32[1,64,64]{2,1,0:T(8,128)S(1)} %get-tuple-element.7), custom_call_target="InvertDiagBlocksLowerTriangular" | custom-call | tf_op jit(solution)/shard_map/triangular_solve | solution.py:12
  155.2 1.9 fusion.34
  157.1 0.0 all-gather.2.cloned.1.call-update
  157.2 0.2 reduce-scatter.5.cloned.1.call-start
  157.4 60.9 %all-gather.2.cloned.1.call-done = f32[64,8192]{1,0:T(8,128)} async-done(((f32[64,512]{1,0:T(8,128)}), f32[64,8192]{1,0:T(8,128)}) %all-gather.2.cloned.1.call-update) | async-done | bytes 2097168 | tf_op jit(solution)/shard_map/all_gather | solution.py:50
  218.3 1.9 copy_bitcast_fusion
  220.2 2.0 gather_fusion.1
  222.2 0.0 copy-start.6
  222.2 10.1 %fusion.17 = f32[64,64,128]{2,0,1:T(8,128)S(1)} fusion(f32[1,1,64,128,128]{4,3,2,1,0:T(8,128)} %param.8, f32[64,64,128]{2,1,0:T(8,128)} %gather_fusion.1, pred[64]{0:T(512)(128)(4,1)S(1)} %get-tuple-element.10), kind=kOutput, calls=%fused_computation.18 | convolution fusion | flops 805830656 | bytes 8388672 | tf_op jit(solution)/shard_map/stb,tab->sta/dot_general | solution.py:54
  232.3 0.0 copy-done.6
  232.3 2.0 fusion.22
  234.3 1.0 copy.44
  235.2 0.0 reduce-scatter.5.cloned.1.call-update
  235.2 6.6 %reduce-scatter.5.cloned.1.call-done = f32[64,1024]{1,0:T(8,128)} async-done(((f32[64,2048]{1,0:T(8,128)}), f32[64,1024]{1,0:T(8,128)}) %reduce-scatter.5.cloned.1.call-update) | async-done | bytes 262160 | tf_op jit(solution)/shard_map/reduce_scatter | solution.py:58
  241.8 0.0 copy-done.2
  241.8 1.4 convolution_subtract_fusion
  243.2 0.4 fusion.54
  243.6 40.7 %psum.15 = f32[64,64]{0,1:T(8,128)S(1)} all-reduce(f32[64,64]{0,1:T(8,128)S(1)} %fusion.54), channel_id=1, replica_groups=mesh['row'=16,'col'=2] {'row','col'}, use_global_device_ids=true, to_apply=%region_5.7 | all-reduce | flops 4096 | bytes 32768 | tf_op jit(solution)/shard_map/psum | solution.py:61
  284.3 0.1 copy.27
  284.4 5.8 %cholesky.55 = f32[64,64]{1,0:T(8,128)S(1)} custom-call(f32[64,64]{1,0:T(8,128)S(1)} %fusion.33), custom_call_target="Cholesky" | custom-call | tf_op jit(solution)/shard_map/jit(cholesky)/cholesky | solution.py:62
  290.3 0.6 compare_reduce_fusion
  290.9 1.3 select_bitcast_fusion
  292.2 4.9 %custom-call.9 = f32[1,64,64]{1,2,0:T(8,128)S(1)} custom-call(f32[1,64,64]{2,1,0:T(8,128)S(1)} %get-tuple-element.5), custom_call_target="InvertDiagBlocksLowerTriangular" | custom-call | tf_op jit(solution)/shard_map/triangular_solve | solution.py:12
  297.1 1.1 fusion.31
  (10 shorter events, 0.2 us)
Async XLA Ops:
  7.2 1.5 copy-start
  7.2 97.6 %reduce-scatter.3.cloned.1.call-start = ((), (), s32[]{:S(2)}) async-start(), calls=%async_computation.2 | async-start | bytes 2228224 | tf_op jit(solution)/shard_map/reduce_scatter | solution.py:46
  10.2 5.7 %copy-start.5 = (s32[1,1,64]{2,1,0:T(1,128)S(1)}, s32[1,1,64]{2,1,0:T(1,128)}, u32[]{:S(2)}) copy-start(s32[1,1,64]{2,1,0:T(1,128)} %param.10) | copy-start | bytes 772
  18.4 1.2 copy-start.3
  18.4 1.2 copy-start.4
  19.9 1.4 copy-start.1
  21.3 197.0 %all-gather.2.cloned.1.call-start = ((), (), s32[]{:S(2)}) async-start(), calls=%async_computation.3 | async-start | bytes 2228224 | tf_op jit(solution)/shard_map/all_gather | solution.py:50
  150.3 91.5 %copy-start.2 = (f32[64,64]{1,0:T(8,128)}, f32[64,64]{1,0:T(8,128)S(1)}, u32[]{:S(2)}) copy-start(f32[64,64]{1,0:T(8,128)S(1)} %get-tuple-element.8) | copy-start | bytes 49156
  157.2 84.7 %reduce-scatter.5.cloned.1.call-start = ((), (), s32[]{:S(2)}) async-start(), calls=%async_computation.4 | async-start | bytes 786432 | tf_op jit(solution)/shard_map/reduce_scatter | solution.py:58
  222.2 10.1 %copy-start.6 = (s32[1,1,64]{2,1,0:T(1,128)S(1)}, s32[1,1,64]{2,1,0:T(1,128)}, u32[]{:S(2)}) copy-start(s32[1,1,64]{2,1,0:T(1,128)} %param.9) | copy-start | bytes 772
Sparse Core Ops, SparseCore 0:
  21.4 83.3 reduce-scatter.2
  157.3 60.9 all-gather.1
  235.4 6.4 reduce-scatter.4
where the time goes:
time: 305 us
  waiting for transfers between devices  151 us (50%)
  blocking collectives  77.7 us (25%)
  other arithmetic  30.1 us (10%)
  matrix products  26.5 us (9%)
  between operations  14 us (5%)
  local copies, waits for them, and re-layouts  5.25 us (2%)
    reduce_scatter x1, waiting for transfers between devices, per_device(): lax.psum_scatter(partial_value, 'row', scatter_dimension=1, tiled=True)  83.4 us
    all_gather x1, waiting for transfers between devices, per_device(): source = lax.all_gather(v_next, 'row', axis=1, tiled=True)  60.9 us
    psum x1, blocking collectives, per_device(): lax.psum(jnp.dot(qt_piece, qt_piece.T, precision=HIGH), ('row', 'col'))  40.7 us
    psum x1, blocking collectives, per_device(): lax.psum(jnp.dot(pt_piece, pt_piece.T, precision=HIGH), ('row', 'col'))  37 us
    another operation x4, other arithmetic, lower_solve(): return lax.linalg.triangular_solve(factor, rhs, left_side=True, lower=True)  11.7 us
    dot_general x1, matrix products, per_device(): products = jnp.einsum('stb,tab->sta', chosen, local_tiles, precision=HIGH)  10.1 us
    reduce_scatter x1, waiting for transfers between devices, per_device(): summed = lax.psum_scatter(terms, 'col', scatter_dimension=1, tiled=True)  6.59 us
    another operation x3, other arithmetic, per_device(): v_factor = jnp.linalg.cholesky(gram / total_cols)  6.52 us
  transfers between devices with their start and end apart: 3, of which 3 were waited for; matrix products, arithmetic and copies ran while one was open for 0% of the time, Pallas kernels for 0%

commit v1 on v0

v1 whole, which is shorter than its diff:
```python
import functools
import math

import jax
import jax.numpy as jnp
from jax import lax
from jax.experimental import pallas as pl
from jax.experimental.pallas import tpu as pltpu
from jax.sharding import PartitionSpec as P

F32 = jnp.float32
BF16 = jnp.bfloat16
HIGH = lax.Precision.HIGHEST
TL = 128
QUADS = 4


def split(x):
    hi = x.astype(BF16)
    return hi, (x - hi.astype(F32)).astype(BF16)


def fold(x):
    w = x.shape[0] // 2
    y = x[:w] + x[w:]
    return y + pltpu.roll(y, w, 1)


def pack(x):
    w = x.shape[0]
    lane = lax.broadcasted_iota(jnp.int32, (w // 2, 2 * w), 1)
    return jnp.where(lane < w, x[: w // 2], x[w // 2 :])


def unpack(x):
    w = x.shape[1] // 2
    lane = lax.broadcasted_iota(jnp.int32, x.shape, 1)
    y = pltpu.roll(x, w, 1)
    return jnp.concatenate([jnp.where(lane < w, x, y), jnp.where(lane < w, y, x)], axis=0)


def factor_pair(gram2):
    w = gram2.shape[0]
    row = lax.broadcasted_iota(jnp.int32, (w, 2 * w), 0)
    lane = lax.broadcasted_iota(jnp.int32, (w, 2 * w), 1)
    m = jnp.where(lane < w, gram2, jnp.where(lane - w == row, 1.0, 0.0).astype(F32))
    below = lax.broadcasted_iota(jnp.int32, (w, 1), 0)
    for j in range(w - 1):
        pivot_row = m[j : j + 1, :]
        inv = 1.0 / m[j : j + 1, j : j + 1]
        times = jnp.where(below > j, m[:, j : j + 1], 0.0)
        m = m - times * (pivot_row * inv)
    diag = jnp.sum(jnp.where(lane == row, m, 0.0), axis=1, keepdims=True)
    m = m * (1.0 / jnp.sqrt(diag))
    return jnp.where((lane >= w) | (lane >= row), m, 0.0)


def transpose_left(pair):
    w = pair.shape[0]
    return jnp.concatenate([pair, pair], axis=0).T[:w, :w]


def kernel(
    nr, nc, total_rows, total_cols,
    idx, tiles, u, expo, v, prior,
    u_out, v_out, vf_out, uf_out,
    u2, part, got, gotz, own, pt, prods, terms, got_terms, gz, g1, g2c, g2q, g2z, qt,
    rs_send, rs_recv, z_send, z_recv, az_send, az_recv, ag_send, ag_recv,
    t_send, t_recv, g1_send, g1_recv, gc_send, gc_recv, gq_send, gq_recv, gg_send, gg_recv,
):
    nz = nr // QUADS
    width = u.shape[0]
    half = width // 2
    rt = terms.shape[0]
    rtc = rt // nc
    tp = part.shape[3]
    each = tiles.shape[0] // rt
    me = lax.axis_index("row")
    mc = lax.axis_index("col")
    z = me // QUADS
    gi = me % QUADS
    gx = gi + 1 - 2 * (gi % 2)
    gy = gi + 2 - 4 * (gi // 2)
    gd = (QUADS - 1) - gi
    base = z * QUADS
    to_x = {"row": base + gx}
    to_y = {"row": base + gy}
    to_d = {"row": base + gd}

    def to_z(zz):
        return {"row": zz * QUADS + gi}

    def to_c(cc):
        return {"col": cc}

    pending = []

    def remote(src, dst, ssem, rsem, dev):
        return pltpu.make_async_remote_copy(
            src_ref=src, dst_ref=dst, send_sem=ssem, recv_sem=rsem, device_id=dev,
            device_id_type=pl.DeviceIdType.MESH,
        )

    def send(*a):
        c = remote(*a)
        c.start()
        pending.append(c)

    barrier = pltpu.get_barrier_semaphore()
    peers = [to_x, to_y, to_d]
    peers += [to_z((z + k) % nz) for k in range(1, nz)]
    peers += [to_c((mc + k) % nc) for k in range(1, nc)]
    for p in peers:
        pl.semaphore_signal(barrier, inc=1, device_id=p, device_id_type=pl.DeviceIdType.MESH)

    for r in range(rt):
        hi, lo = split(u[:, r * TL : (r + 1) * TL])
        u2[r, 0:width] = hi
        u2[r, width : 2 * width] = lo

    def left_tile(j):
        th, tl_ = split(tiles[idx[0, j]])
        both = jnp.concatenate([th, tl_], axis=1)
        x = jnp.dot(u2[idx[1, j]], both, preferred_element_type=F32)
        y = x[:width] + x[width:]
        return y[:, :TL] + y[:, TL:]

    def compute(k):
        zz = (z + 1 + k) % nz
        for n, q in enumerate((gd, gx, gy, gi)):
            def body(t, _, q=q):
                y = left_tile((zz * QUADS + q) * tp + t)
                part[zz, q, 0, t] = y[:half]
                part[zz, q, 1, t] = y[half:]
                return 0
            lax.fori_loop(0, tp, body, 0, unroll=True)
            if n == 0 and k == 0:
                pl.semaphore_wait(barrier, len(peers))
            if n == 0:
                send(part.at[zz, q, 0], got.at[k, 0], rs_send.at[k, 0], rs_recv.at[k, 0], to_x)
                send(part.at[zz, q, 1], got.at[k, 1], rs_send.at[k, 1], rs_recv.at[k, 1], to_y)
            elif n == 1:
                send(part.at[zz, q, 0], got.at[k, 2], rs_send.at[k, 2], rs_recv.at[k, 2], to_x)
            elif n == 2:
                send(part.at[zz, q, 1], got.at[k, 3], rs_send.at[k, 3], rs_recv.at[k, 3], to_y)

    def rs_wait(k, n):
        remote(got.at[k, n], got.at[k, n], rs_send.at[k, n], rs_recv.at[k, n], to_x).wait_recv()

    def step2(k):
        zz = (z + 1 + k) % nz
        rs_wait(k, 0)
        part[zz, gy, 0] = part[zz, gy, 0] + got[k, 0]
        send(part.at[zz, gy, 0], got.at[k, 4], rs_send.at[k, 4], rs_recv.at[k, 4], to_y)
        rs_wait(k, 1)
        part[zz, gx, 1] = part[zz, gx, 1] + got[k, 1]
        send(part.at[zz, gx, 1], got.at[k, 5], rs_send.at[k, 5], rs_recv.at[k, 5], to_x)

    def step3(k):
        zz = (z + 1 + k) % nz
        for n in (2, 3, 4, 5):
            rs_wait(k, n)
        part[zz, gi, 0] = part[zz, gi, 0] + (got[k, 2] + got[k, 4])
        part[zz, gi, 1] = part[zz, gi, 1] + (got[k, 3] + got[k, 5])
        if k < nz - 1:
            send(part.at[zz, gi], gotz.at[z], z_send.at[k], z_recv.at[z], to_z(zz))

    for k in range(nz + 2):
        if k < nz:
            compute(k)
        if k == 0:
            tri = lax.broadcasted_iota(jnp.int32, prior.shape, 0) >= lax.broadcasted_iota(
                jnp.int32, prior.shape, 1
            )
            low = jnp.where(tri, prior[...], 0.0)
            own[...] = jnp.dot(low, v[...], precision=HIGH, preferred_element_type=F32)
        if 1 <= k < nz + 1:
            step2(k - 1)
        if 2 <= k:
            step3(k - 2)

    def scale_of(j):
        e = expo[j]
        return jnp.where(e % 2 == 1, 0.5, 1.0) * jnp.where(e >= 2, 0.25, 1.0)

    for k in range(1, nz):
        zs = (z + k) % nz
        remote(gotz.at[zs], gotz.at[zs], z_send.at[k - 1], z_recv.at[zs], to_z(zs)).wait_recv()
    for t in range(tp):
        sc = scale_of(me * tp + t)
        for h in range(2):
            x = part[z, gi, h, t]
            for k in range(1, nz):
                x = x + gotz[(z + k) % nz, h, t]
            pt[z, gi, h, t] = x * sc - own[h * half : (h + 1) * half, t * TL : (t + 1) * TL]

    for k in range(1, nz):
        zs = (z + k) % nz
        send(pt.at[z, gi], pt.at[z, gi], az_send.at[k - 1], az_recv.at[z], to_z(zs))

    def ag(src, k, n, dev):
        send(src, src, ag_send.at[k, n], ag_recv.at[k, n], dev)

    def ag_wait(dst, k, n):
        remote(dst, dst, ag_send.at[k, n], ag_recv.at[k, n], to_x).wait_recv()

    def right_tiles(zz, q):
        def body(t, acc):
            j = (zz * QUADS + q) * tp + t
            x = jnp.concatenate([pt[zz, q, 0, t], pt[zz, q, 1, t]], axis=0)
            hi, lo = split(x)
            xx = jnp.concatenate([hi, lo], axis=0)
            acc = acc + lax.dot_general(
                xx, xx, (((1,), (1,)), ((), ())), preferred_element_type=F32
            )
            th, tl_ = split(tiles[idx[0, j]])
            both = jnp.concatenate([th, tl_], axis=0)
            xs = (xx.astype(F32) * scale_of(j)).astype(BF16)
            y = lax.dot_general(xs, both, (((1,), (1,)), ((), ())), preferred_element_type=F32)
            y = y[:width] + y[width:]
            prods[j] = y[:, :TL] + y[:, TL:]
            return acc
        gz[zz * QUADS + q] = lax.fori_loop(
            0, tp, body, jnp.zeros((2 * width, 2 * width), F32), unroll=True
        )

    def arrive(k):
        zs = (z + nz - k) % nz
        if k:
            remote(pt.at[zs, gi], pt.at[zs, gi], az_send.at[0], az_recv.at[zs], to_z(zs)).wait_recv()
        ag(pt.at[zs, gi, 0], k, 0, to_y)
        ag(pt.at[zs, gi, 1], k, 1, to_x)
        ag(pt.at[zs, gi, 0], k, 2, to_x)
        ag(pt.at[zs, gi, 1], k, 3, to_y)
        right_tiles(zs, gi)

    def relay(k):
        zs = (z + nz - k) % nz
        ag_wait(pt.at[zs, gy, 0], k, 0)
        ag(pt.at[zs, gy, 0], k, 4, to_x)
        ag_wait(pt.at[zs, gx, 1], k, 1)
        ag(pt.at[zs, gx, 1], k, 5, to_y)

    def finish(k):
        zs = (z + nz - k) % nz
        ag_wait(pt.at[zs, gx, 0], k, 2)
        right_tiles(zs, gx)
        ag_wait(pt.at[zs, gy, 1], k, 3)
        right_tiles(zs, gy)
        ag_wait(pt.at[zs, gd, 0], k, 4)
        ag_wait(pt.at[zs, gd, 1], k, 5)
        right_tiles(zs, gd)

    for k in range(nz + 2):
        if k < nz:
            arrive(k)
        if 1 <= k < nz + 1:
            relay(k - 1)
        if 2 <= k:
            finish(k - 2)

    g = lax.fori_loop(
        1, nr, lambda i, a: a + gz[i], gz[0]
    )
    g1[mc] = pack(fold(g))
    for k in range(1, nc):
        cc = (mc + k) % nc
        send(g1.at[mc], g1.at[mc], g1_send.at[k - 1], g1_recv.at[mc], to_c(cc))

    def row_terms(r, _):
        x = prods[idx[2, r * each]]
        for i in range(1, each):
            x = x + prods[idx[2, r * each + i]]
        terms[r] = x
        return 0
    lax.fori_loop(0, rt, row_terms, 0)
    for k in range(1, nc):
        cc = (mc + k) % nc
        send(terms.at[pl.ds(cc * rtc, rtc)], got_terms.at[mc], t_send.at[k - 1], t_recv.at[mc], to_c(cc))

    for k in range(1, nc):
        cc = (mc + k) % nc
        remote(g1.at[cc], g1.at[cc], g1_send.at[k - 1], g1_recv.at[cc], to_c(cc)).wait_recv()
    gs = g1[0]
    for cc in range(1, nc):
        gs = gs + g1[cc]
    pair = factor_pair(unpack(gs * (1.0 / total_cols)))
    vf_out[...] = transpose_left(pair)
    for t in range(tp):
        x = jnp.concatenate(
            [jnp.zeros((width, TL), F32), pt[z, gi, 0, t], pt[z, gi, 1, t]], axis=0
        )
        v_out[:, t * TL : (t + 1) * TL] = jnp.dot(
            pair, x, precision=HIGH, preferred_element_type=F32
        )

    for k in range(1, nc):
        cc = (mc + k) % nc
        remote(got_terms.at[cc], got_terms.at[cc], t_send.at[k - 1], t_recv.at[cc], to_c(cc)).wait_recv()
    root = math.sqrt(total_rows / total_cols)

    acc = jnp.zeros((2 * width, 2 * width), F32)
    for i in range(rtc):
        r = mc * rtc + i
        x = terms[r]
        for k in range(1, nc):
            x = x + got_terms[(mc + k) % nc, i]
        uu = u[:, pl.ds(pl.multiple_of(r * TL, TL), TL)]
        q = jnp.dot(
            pair, jnp.concatenate([-uu, root * x], axis=0), precision=HIGH, preferred_element_type=F32
        )
        qt[i] = q
        xx = jnp.concatenate(split(q), axis=0)
        acc = acc + lax.dot_general(xx, xx, (((1,), (1,)), ((), ())), preferred_element_type=F32)

    def sum_over(buf, mine, n, x, ssem, rsem, to):
        buf[mine] = x
        for k in range(1, n):
            send(buf.at[mine], buf.at[mine], ssem.at[k - 1], rsem.at[mine], to((mine + k) % n))
        for k in range(1, n):
            o = (mine + k) % n
            remote(buf.at[o], buf.at[o], ssem.at[k - 1], rsem.at[o], to(o)).wait_recv()
        y = buf[0]
        for o in range(1, n):
            y = y + buf[o]
        return y

    x = sum_over(g2c, mc, nc, pack(fold(acc)), gc_send, gc_recv, to_c)
    x = sum_over(g2q, gi, QUADS, x, gq_send, gq_recv, lambda q: {"row": base + q})
    x = sum_over(g2z, z, nz, x, gg_send, gg_recv, to_z)
    pair2 = factor_pair(unpack(x * (1.0 / total_rows)))
    uf_out[...] = transpose_left(pair2)
    for i in range(rtc):
        y = jnp.concatenate([jnp.zeros((width, TL), F32), qt[i]], axis=0)
        u_out[:, i * TL : (i + 1) * TL] = jnp.dot(
            pair2, y, precision=HIGH, preferred_element_type=F32
        )
    for c in pending:
        c.wait_send()


def per_device(tiles, tile_rows, tile_cols, exponents, u_basis, v_basis, prior):
    nr, nc = lax.axis_size("row"), lax.axis_size("col")
    nz = nr // QUADS
    local = tiles[0, 0]
    rows, cols = tile_rows[0, 0], tile_cols[0, 0]
    count = local.shape[0]
    width, block_rows = u_basis.shape
    block_cols = exponents.shape[0]
    rt, ct = block_rows // TL, block_cols // TL
    tp = ct // nr
    rtc = rt // nc
    half = width // 2
    k = jnp.arange(count, dtype=jnp.int32)
    hit = cols[:, None] == k[None, :]
    key = rows * count + k
    rank = jnp.sum((key[None, :] < key[:, None]).astype(jnp.int32), axis=1)
    place = rank[:, None] == k[None, :]
    idx = jnp.stack([
        jnp.sum(jnp.where(hit, k[:, None], 0), axis=0),
        jnp.sum(jnp.where(hit, rows[:, None], 0), axis=0),
        jnp.sum(jnp.where(place, cols[:, None], 0), axis=0),
    ])
    expo = exponents.reshape(ct, 1, TL)
    dma = pltpu.SemaphoreType.DMA
    vm = pl.BlockSpec(memory_space=pltpu.VMEM)

    def sems(*shape):
        return [dma(shape), dma(shape)]

    return pl.pallas_call(
        functools.partial(kernel, nr, nc, block_rows * nr, block_cols * nc),
        out_shape=(
            jax.ShapeDtypeStruct((width, block_rows // nc), F32),
            jax.ShapeDtypeStruct((width, block_cols // nr), F32),
            jax.ShapeDtypeStruct((width, width), F32),
            jax.ShapeDtypeStruct((width, width), F32),
        ),
        in_specs=[pl.BlockSpec(memory_space=pltpu.SMEM)] + [vm] * 5,
        out_specs=(vm,) * 4,
        scratch_shapes=[
            pltpu.VMEM((rt, 2 * width, TL), BF16),
            pltpu.VMEM((nz, QUADS, 2, tp, half, TL), F32),
            pltpu.VMEM((nz, 6, tp, half, TL), F32),
            pltpu.VMEM((nz, 2, tp, half, TL), F32),
            pltpu.VMEM((width, tp * TL), F32),
            pltpu.VMEM((nz, QUADS, 2, tp, half, TL), F32),
            pltpu.VMEM((ct, width, TL), F32),
            pltpu.VMEM((rt, width, TL), F32),
            pltpu.VMEM((nc, rtc, width, TL), F32),
            pltpu.VMEM((nr, 2 * width, 2 * width), F32),
            pltpu.VMEM((nc, half, 2 * width), F32),
            pltpu.VMEM((nc, half, 2 * width), F32),
            pltpu.VMEM((QUADS, half, 2 * width), F32),
            pltpu.VMEM((nz, half, 2 * width), F32),
            pltpu.VMEM((rtc, width, TL), F32),
            *sems(nz, 6),
            dma((nz,)), dma((nz,)),
            dma((nz,)), dma((nz,)),
            *sems(nz, 6),
            dma((nc,)), dma((nc,)),
            dma((nc,)), dma((nc,)),
            dma((nc,)), dma((nc,)),
            dma((QUADS,)), dma((QUADS,)),
            dma((nz,)), dma((nz,)),
        ],
        compiler_params=pltpu.CompilerParams(
            collective_id=0, has_side_effects=True, vmem_limit_bytes=48 * 1024 * 1024
        ),
    )(idx, local, u_basis, expo, v_basis, prior)


def solution(mesh):
    placed = (
        P("row", "col", None, None, None),
        P("row", "col", None),
        P("row", "col", None),
        P("col"),
        P(None, "row"),
        P(None, ("col", "row")),
        P(),
    )
    return jax.shard_map(
        per_device,
        mesh=mesh,
        in_specs=placed,
        out_specs=(P(None, ("row", "col")), P(None, ("col", "row")), P(), P()),
        check_vma=False,
    )
```

time: 305 us -> 86.7 us (0.28)
  waiting for transfers between devices: 151 us -> 0 us
  blocking collectives: 77.7 us -> 0 us
  Pallas kernels: 0 us -> 75.8 us
  other arithmetic: 30.1 us -> 1.63 us
  matrix products: 26.5 us -> 0 us
  between operations: 14 us -> 0.67 us
    reduce_scatter x2 -> x0, waiting for transfers between devices: 90 us -> none  [the longest x1 83.4 us: per_device(): lax.psum_scatter(partial_value, 'row', scatter_dimension=1, tiled=True)]
    psum x2 -> x0, blocking collectives: 77.7 us -> none  [the longest x1 40.7 us: per_device(): lax.psum(jnp.dot(qt_piece, qt_piece.T, precision=HIGH), ('row', 'col'))]
    pallas_call x0 -> x1, Pallas kernels: none -> 75.8 us  [per_device(): pl.pallas_call(functools.partial(kernel, nr, nc, block_rows * nr, block_c...]
    all_gather x1 -> x0, waiting for transfers between devices: 60.9 us -> none  [per_device(): source = lax.all_gather(v_next, 'row', axis=1, tiled=True)]
    another operation x10 -> x1, other arithmetic: 24.8 us -> 0.01 us  [per_device(): jnp.stack([jnp.sum(jnp.where(hit, k[:, None], 0), axis=0), jnp.sum(jnp.wh...]
    dot_general x8 -> x0, matrix products: 23.4 us -> none  [the longest x1 10.1 us: per_device(): products = jnp.einsum('stb,tab->sta', chosen, local_tiles, precision=HIGH)]
    unnamed x15 -> x14, local copies, waits for them, and re-layouts: 2.33 us -> 8.23 us
  transfers between devices with their start and end apart: 3 -> 0, of which waited for: 3 -> 0; matrix products, arithmetic and copies ran while one was open for 0% -> 0% of each run, Pallas kernels for 0% -> 0%
where the time goes in v1:
time: 86.7 us; the launch traced here: 86.3 us
  Pallas kernels  75.8 us (87%)
  local copies, waits for them, and re-layouts  8.23 us (9%)
  other arithmetic  1.63 us (2%)
    pallas_call x1, Pallas kernels, per_device(): pl.pallas_call(functools.partial(kernel, nr, nc, block_rows * nr, block_c...  75.8 us
    unnamed x14, local copies, waits for them, and re-layouts  8.23 us

profile of v1, /device:TPU:0, one launch (start us, length us, event | category | flops | bytes accessed | tf_op | source)
XLA Modules:
  0.0 86.3 jit_solution(9645642346499880624)
XLA Ops:
  0.6 0.7 iota_add_fusion
  1.3 0.2 convert_reduce_fusion
  1.5 0.8 select_reduce_fusion.2
  2.3 0.0 copy-start
  2.3 2.2 %copy-done = f32[1,1,64,128,128]{4,3,2,1,0:T(8,128)S(1)} copy-done((f32[1,1,64,128,128]{4,3,2,1,0:T(8,128)S(1)}, f32[1,1,64,128,128]{4,3,2,1,0:T(8,128)}, u32[]{:S(2)}) %copy-start) | copy-done | bytes 4194328
  4.5 0.0 copy-start.1
  4.5 1.0 %copy-done.1 = f32[64,2048]{1,0:T(8,128)S(1)} copy-done((f32[64,2048]{1,0:T(8,128)S(1)}, f32[64,2048]{1,0:T(8,128)}, u32[]{:S(2)}) %copy-start.1) | copy-done | bytes 524312
  5.5 0.0 copy-start.2
  5.5 0.9 %copy-done.2 = f32[64,512]{1,0:T(8,128)S(1)} copy-done((f32[64,512]{1,0:T(8,128)S(1)}, f32[64,512]{1,0:T(8,128)}, u32[]{:S(2)}) %copy-start.2) | copy-done | bytes 131096
  6.4 0.0 copy-start.3
  6.4 0.8 copy-done.3
  7.2 0.0 copy-start.4
  7.2 0.8 copy-done.4
  7.9 75.8 %shard_map.102 = (f32[64,1024]{1,0:T(8,128)S(1)}, f32[64,512]{1,0:T(8,128)S(1)}, f32[64,64]{1,0:T(8,128)S(1)}, f32[64,64]{1,0:T(8,128)S(1)}) custom-call(s32[3,64]{1,0:T(4,128)S(1)} %pad_add_fusion.idx, f32[64,128,128]{2,1,0:T(8,128)S(1)} %bitcast.8, f32[64,2048]{1,0:T(8,128)S(1)} %copy-done.1, s32[64,1,128]{2,1,0:T(1,128)S(1)} %bitcast.9, ...), custom_call_target="tpu_custom_call" | custom-call | tf_op jit(solution)/shard_map/pallas_call | solution.py:371
  83.8 0.7 copy.15
  84.5 0.7 copy.16
  85.1 0.6 copy.17
  85.7 0.6 copy.18
  (1 shorter events, 0.0 us)
Async XLA Ops:
  2.3 2.2 %copy-start = (f32[1,1,64,128,128]{4,3,2,1,0:T(8,128)S(1)}, f32[1,1,64,128,128]{4,3,2,1,0:T(8,128)}, u32[]{:S(2)}) copy-start(f32[1,1,64,128,128]{4,3,2,1,0:T(8,128)} %param.7) | copy-start | bytes 12582916
  4.5 1.0 %copy-start.1 = (f32[64,2048]{1,0:T(8,128)S(1)}, f32[64,2048]{1,0:T(8,128)}, u32[]{:S(2)}) copy-start(f32[64,2048]{1,0:T(8,128)} %u.1) | copy-start | bytes 1572868
  5.5 0.9 %copy-start.2 = (f32[64,512]{1,0:T(8,128)S(1)}, f32[64,512]{1,0:T(8,128)}, u32[]{:S(2)}) copy-start(f32[64,512]{1,0:T(8,128)} %v.1) | copy-start | bytes 393220
  6.4 0.8 copy-start.3
  7.2 0.8 copy-start.4

commit v2 on v1

--- a/solution.py
+++ b/solution.py
@@ -39,17 +39,32 @@
     return jnp.concatenate([jnp.where(lane < w, x, y), jnp.where(lane < w, y, x)], axis=0)
 
 
-def factor_pair(gram2):
+def factor_pair(gram2, block=4):
     w = gram2.shape[0]
     row = lax.broadcasted_iota(jnp.int32, (w, 2 * w), 0)
     lane = lax.broadcasted_iota(jnp.int32, (w, 2 * w), 1)
     m = jnp.where(lane < w, gram2, jnp.where(lane - w == row, 1.0, 0.0).astype(F32))
-    below = lax.broadcasted_iota(jnp.int32, (w, 1), 0)
-    for j in range(w - 1):
-        pivot_row = m[j : j + 1, :]
-        inv = 1.0 / m[j : j + 1, j : j + 1]
-        times = jnp.where(below > j, m[:, j : j + 1], 0.0)
-        m = m - times * (pivot_row * inv)
+    done, top = [], 0
+    for j in range(0, w, block):
+        o = j - top
+        below = row[top:]
+        cols = [jnp.broadcast_to(m[:, j + i : j + i + 1], m.shape) for i in range(block)]
+        rows = [m[o + i : o + i + 1] for i in range(block)]
+        a = {(i, l): cols[l][o + i : o + i + 1] for i in range(block) for l in range(i, block)}
+        for i in range(block):
+            inv = 1.0 / a[i, i]
+            m = m - jnp.where(below > j + i, cols[i], 0.0) * (rows[i] * inv)
+            for l in range(i + 1, block):
+                s = a[i, l] * inv
+                rows[l] = rows[l] - s * rows[i]
+                cols[l] = cols[l] - s * cols[i]
+                for q in range(l, block):
+                    a[l, q] = a[l, q] - s * a[i, q]
+        if (j + block) % 8 == 0:
+            done.append(m[:8])
+            m = m[8:]
+            top += 8
+    m = jnp.concatenate(done, axis=0)
     diag = jnp.sum(jnp.where(lane == row, m, 0.0), axis=1, keepdims=True)
     m = m * (1.0 / jnp.sqrt(diag))
     return jnp.where((lane >= w) | (lane >= row), m, 0.0)
@@ -60,10 +75,30 @@
     return jnp.concatenate([pair, pair], axis=0).T[:w, :w]
 
 
+def tile_lists(rows_in, cols_in, lists, row_count, col_count):
+    n = rows_in.shape[1]
+    rows = jnp.broadcast_to(rows_in[...], (n, n))
+    cols = jnp.broadcast_to(cols_in[...], (n, n))
+    down = lax.broadcasted_iota(jnp.int32, (n, n), 0)
+    across = lax.broadcasted_iota(jnp.int32, (n, n), 1)
+    key = rows * n + across
+    key_down = jnp.sum(jnp.where(down == across, key, 0), axis=1, keepdims=True)
+    rank = jnp.sum(jnp.where(key_down < key, 1, 0), axis=0, keepdims=True)
+    hit = cols == down
+    tile = jnp.max(jnp.where(hit, across, 0), axis=1, keepdims=True)
+    tile_row = jnp.clip(jnp.max(jnp.where(hit, rows, 0), axis=1, keepdims=True), 0, row_count - 1)
+    ordered = jnp.clip(
+        jnp.max(jnp.where(rank == down, cols, 0), axis=1, keepdims=True), 0, col_count - 1
+    )
+    lane = lax.broadcasted_iota(jnp.int32, lists.shape, 1)
+    lists[...] = jnp.where(lane == 0, tile, jnp.where(lane == 1, tile_row, ordered))
+
+
 def kernel(
     nr, nc, total_rows, total_cols,
-    idx, tiles, u, expo, v, prior,
+    rows_hbm, cols_hbm, tiles_hbm, u_hbm, expo_hbm, v_hbm, prior_hbm,
     u_out, v_out, vf_out, uf_out,
+    rows_in, cols_in, tiles, u, expo, v, prior, lists, idx, in_sem,
     u2, part, got, gotz, own, pt, prods, terms, got_terms, gz, g1, g2c, g2q, g2z, qt,
     rs_send, rs_recv, z_send, z_recv, az_send, az_recv, ag_send, ag_recv,
     t_send, t_recv, g1_send, g1_recv, gc_send, gc_recv, gq_send, gq_recv, gg_send, gg_recv,
@@ -106,6 +141,15 @@
         c.start()
         pending.append(c)
 
+    fetch = [
+        pltpu.make_async_copy(src, dst, in_sem.at[i])
+        for i, (src, dst) in enumerate((
+            (rows_hbm, rows_in), (cols_hbm, cols_in), (u_hbm, u), (tiles_hbm, tiles),
+            (expo_hbm, expo), (v_hbm, v), (prior_hbm, prior),
+        ))
+    ]
+    for c in fetch:
+        c.start()
     barrier = pltpu.get_barrier_semaphore()
     peers = [to_x, to_y, to_d]
     peers += [to_z((z + k) % nz) for k in range(1, nz)]
@@ -113,15 +157,25 @@
     for p in peers:
         pl.semaphore_signal(barrier, inc=1, device_id=p, device_id_type=pl.DeviceIdType.MESH)
 
+    for c in fetch[:2]:
+        c.wait()
+    tile_lists(rows_in, cols_in, lists, rt, expo.shape[0])
+    to_scalars = pltpu.make_async_copy(lists, idx, in_sem.at[len(fetch)])
+    to_scalars.start()
+    fetch[2].wait()
     for r in range(rt):
         hi, lo = split(u[:, r * TL : (r + 1) * TL])
         u2[r, 0:width] = hi
         u2[r, width : 2 * width] = lo
 
+    to_scalars.wait()
+    for c in fetch[3:]:
+        c.wait()
+
     def left_tile(j):
-        th, tl_ = split(tiles[idx[0, j]])
+        th, tl_ = split(tiles[idx[j, 0]])
         both = jnp.concatenate([th, tl_], axis=1)
-        x = jnp.dot(u2[idx[1, j]], both, preferred_element_type=F32)
+        x = jnp.dot(u2[idx[j, 1]], both, preferred_element_type=F32)
         y = x[:width] + x[width:]
         return y[:, :TL] + y[:, TL:]
 
@@ -213,7 +267,7 @@
             acc = acc + lax.dot_general(
                 xx, xx, (((1,), (1,)), ((), ())), preferred_element_type=F32
             )
-            th, tl_ = split(tiles[idx[0, j]])
+            th, tl_ = split(tiles[idx[j, 0]])
             both = jnp.concatenate([th, tl_], axis=0)
             xs = (xx.astype(F32) * scale_of(j)).astype(BF16)
             y = lax.dot_general(xs, both, (((1,), (1,)), ((), ())), preferred_element_type=F32)
@@ -268,9 +322,9 @@
         send(g1.at[mc], g1.at[mc], g1_send.at[k - 1], g1_recv.at[mc], to_c(cc))
 
     def row_terms(r, _):
-        x = prods[idx[2, r * each]]
+        x = prods[idx[r * each, 2]]
         for i in range(1, each):
-            x = x + prods[idx[2, r * each + i]]
+            x = x + prods[idx[r * each + i, 2]]
         terms[r] = x
         return 0
     lax.fori_loop(0, rt, row_terms, 0)
@@ -343,7 +397,7 @@
     nr, nc = lax.axis_size("row"), lax.axis_size("col")
     nz = nr // QUADS
     local = tiles[0, 0]
-    rows, cols = tile_rows[0, 0], tile_cols[0, 0]
+    rows, cols = tile_rows[0], tile_cols[0]
     count = local.shape[0]
     width, block_rows = u_basis.shape
     block_cols = exponents.shape[0]
@@ -351,16 +405,6 @@
     tp = ct // nr
     rtc = rt // nc
     half = width // 2
-    k = jnp.arange(count, dtype=jnp.int32)
-    hit = cols[:, None] == k[None, :]
-    key = rows * count + k
-    rank = jnp.sum((key[None, :] < key[:, None]).astype(jnp.int32), axis=1)
-    place = rank[:, None] == k[None, :]
-    idx = jnp.stack([
-        jnp.sum(jnp.where(hit, k[:, None], 0), axis=0),
-        jnp.sum(jnp.where(hit, rows[:, None], 0), axis=0),
-        jnp.sum(jnp.where(place, cols[:, None], 0), axis=0),
-    ])
     expo = exponents.reshape(ct, 1, TL)
     dma = pltpu.SemaphoreType.DMA
     vm = pl.BlockSpec(memory_space=pltpu.VMEM)
@@ -376,9 +420,19 @@
             jax.ShapeDtypeStruct((width, width), F32),
             jax.ShapeDtypeStruct((width, width), F32),
         ),
-        in_specs=[pl.BlockSpec(memory_space=pltpu.SMEM)] + [vm] * 5,
+        in_specs=[pl.BlockSpec(memory_space=pl.ANY)] * 7,
         out_specs=(vm,) * 4,
         scratch_shapes=[
+            pltpu.VMEM((1, count), jnp.int32),
+            pltpu.VMEM((1, count), jnp.int32),
+            pltpu.VMEM((count, TL, TL), F32),
+            pltpu.VMEM((width, block_rows), F32),
+            pltpu.VMEM((ct, 1, TL), jnp.int32),
+            pltpu.VMEM((width, tp * TL), F32),
+            pltpu.VMEM((width, width), F32),
+            pltpu.VMEM((count, TL), jnp.int32),
+            pltpu.SMEM((count, TL), jnp.int32),
+            dma((8,)),
             pltpu.VMEM((rt, 2 * width, TL), BF16),
             pltpu.VMEM((nz, QUADS, 2, tp, half, TL), F32),
             pltpu.VMEM((nz, 6, tp, half, TL), F32),
@@ -405,9 +459,9 @@
             dma((nz,)), dma((nz,)),
         ],
         compiler_params=pltpu.CompilerParams(
-            collective_id=0, has_side_effects=True, vmem_limit_bytes=48 * 1024 * 1024
+            collective_id=0, has_side_effects=True, vmem_limit_bytes=56 * 1024 * 1024
         ),
-    )(idx, local, u_basis, expo, v_basis, prior)
+    )(rows, cols, local, u_basis, expo, v_basis, prior)
 
 
 def solution(mesh):

time: 86.7 us -> 77.3 us (0.89)
  Pallas kernels: 75.8 us -> 70.4 us
  local copies, waits for them, and re-layouts: 8.23 us -> 5.99 us
  other arithmetic: 1.63 us -> 0 us
    pallas_call x1, Pallas kernels: 75.8 us -> 70.4 us  [per_device(): pl.pallas_call(functools.partial(kernel, nr, nc, block_rows * nr, block_c...]
    unnamed x14 -> x4, local copies, waits for them, and re-layouts: 8.23 us -> 5.99 us
    reduce_sum x2 -> x0, other arithmetic: 0.96 us -> none  [the longest x1 0.78 us: per_device(): jnp.sum(jnp.where(hit, k[:, None], 0), axis=0)]
where the time goes in v2:
time: 77.3 us; the launch traced here: 77 us
  Pallas kernels  70.4 us (91%)
  local copies, waits for them, and re-layouts  5.99 us (8%)
    pallas_call x1, Pallas kernels, per_device(): pl.pallas_call(functools.partial(kernel, nr, nc, block_rows * nr, block_c...  70.4 us
    unnamed x4, local copies, waits for them, and re-layouts  5.99 us

profile of v2, /device:TPU:0, one launch (start us, length us, event | category | flops | bytes accessed | tf_op | source)
XLA Modules:
  0.0 77.0 jit_solution(7268898799292708757)
XLA Ops:
  0.6 70.4 %shard_map.102 = (f32[64,1024]{1,0:T(8,128)}, f32[64,512]{1,0:T(8,128)}, f32[64,64]{1,0:T(8,128)}, f32[64,64]{1,0:T(8,128)}) custom-call(s32[1,64]{1,0:T(1,128)} %bitcast.6, s32[1,64]{1,0:T(1,128)} %bitcast.7, f32[64,128,128]{2,1,0:T(8,128)} %bitcast.4, f32[64,2048]{1,0:T(8,128)} %u_hbm.1, s32[64,1,128]{2,1,0:T(1,128)} %bitcast.5, f32[64,512]{1,0:T(8,128)} %v_hbm.1, ...), custom_call_target="tpu_custom_call" | custom-call | tf_op jit(solution)/shard_map/pallas_call | solution.py:415
  71.0 1.7 %copy.15 = f32[64,1024]{1,0:T(8,128)} copy(f32[64,1024]{1,0:T(8,128)} %get-tuple-element.8) | data formatting | bytes 524288
  72.7 1.6 %copy.16 = f32[64,512]{1,0:T(8,128)} copy(f32[64,512]{1,0:T(8,128)} %get-tuple-element.9) | data formatting | bytes 262144
  74.3 1.4 %copy.17 = f32[64,64]{1,0:T(8,128)} copy(f32[64,64]{1,0:T(8,128)} %get-tuple-element.10) | data formatting | bytes 32768
  75.6 1.4 %copy.18 = f32[64,64]{1,0:T(8,128)} copy(f32[64,64]{1,0:T(8,128)} %get-tuple-element.11) | data formatting | bytes 32768

commit v3 on v2

--- a/solution.py
+++ b/solution.py
@@ -99,9 +99,10 @@
     rows_hbm, cols_hbm, tiles_hbm, u_hbm, expo_hbm, v_hbm, prior_hbm,
     u_out, v_out, vf_out, uf_out,
     rows_in, cols_in, tiles, u, expo, v, prior, lists, idx, in_sem,
-    u2, part, got, gotz, own, pt, prods, terms, got_terms, gz, g1, g2c, g2q, g2z, qt,
+    u2, part, got, gotz, own, pt, prods, terms, got_terms, g1c, g1q, g1z, g2c, g2q, g2z, qt, pair_ref,
     rs_send, rs_recv, z_send, z_recv, az_send, az_recv, ag_send, ag_recv,
-    t_send, t_recv, g1_send, g1_recv, gc_send, gc_recv, gq_send, gq_recv, gg_send, gg_recv,
+    t_send, t_recv, c1_send, c1_recv, q1_send, q1_recv, z1_send, z1_recv,
+    c2_send, c2_recv, q2_send, q2_recv, z2_send, z2_recv,
 ):
     nz = nr // QUADS
     width = u.shape[0]
@@ -259,24 +260,26 @@
         remote(dst, dst, ag_send.at[k, n], ag_recv.at[k, n], to_x).wait_recv()
 
     def right_tiles(zz, q):
-        def body(t, acc):
+        for t in range(tp):
             j = (zz * QUADS + q) * tp + t
             x = jnp.concatenate([pt[zz, q, 0, t], pt[zz, q, 1, t]], axis=0)
-            hi, lo = split(x)
-            xx = jnp.concatenate([hi, lo], axis=0)
+            xs = jnp.concatenate(split(x * scale_of(j)), axis=0)
+            both = jnp.concatenate(split(tiles[idx[j, 0]]), axis=0)
+            y = lax.dot_general(xs, both, (((1,), (1,)), ((), ())), preferred_element_type=F32)
+            y = y[:width] + y[width:]
+            prods[j] = y[:, :TL] + y[:, TL:]
+
+    def gram_of(parts):
+        acc = jnp.zeros((2 * width, 2 * width), F32)
+        for x in parts:
+            xx = jnp.concatenate(split(x), axis=0)
             acc = acc + lax.dot_general(
                 xx, xx, (((1,), (1,)), ((), ())), preferred_element_type=F32
             )
-            th, tl_ = split(tiles[idx[j, 0]])
-            both = jnp.concatenate([th, tl_], axis=0)
-            xs = (xx.astype(F32) * scale_of(j)).astype(BF16)
-            y = lax.dot_general(xs, both, (((1,), (1,)), ((), ())), preferred_element_type=F32)
-            y = y[:width] + y[width:]
-            prods[j] = y[:, :TL] + y[:, TL:]
-            return acc
-        gz[zz * QUADS + q] = lax.fori_loop(
-            0, tp, body, jnp.zeros((2 * width, 2 * width), F32), unroll=True
-        )
+        return pack(fold(acc))
+
+    def own_tile(t):
+        return jnp.concatenate([pt[z, gi, 0, t], pt[z, gi, 1, t]], axis=0)
 
     def arrive(k):
         zs = (z + nz - k) % nz
@@ -305,6 +308,52 @@
         ag_wait(pt.at[zs, gd, 1], k, 5)
         right_tiles(zs, gd)
 
+    def sum_start(buf, mine, n, x, ssem, rsem, to):
+        buf[mine] = x
+        for k in range(1, n):
+            send(buf.at[mine], buf.at[mine], ssem.at[k - 1], rsem.at[mine], to((mine + k) % n))
+
+    def sum_end(buf, mine, n, ssem, rsem, to):
+        for k in range(1, n):
+            o = (mine + k) % n
+            remote(buf.at[o], buf.at[o], ssem.at[k - 1], rsem.at[o], to(o)).wait_recv()
+        y = buf[0]
+        for o in range(1, n):
+            y = y + buf[o]
+        return y
+
+    def to_q(q):
+        return {"row": base + q}
+
+    first = (
+        (g1c, mc, nc, c1_send, c1_recv, to_c),
+        (g1q, gi, QUADS, q1_send, q1_recv, to_q),
+        (g1z, z, nz, z1_send, z1_recv, to_z),
+    )
+    second = (
+        (g2c, mc, nc, c2_send, c2_recv, to_c),
+        (g2q, gi, QUADS, q2_send, q2_recv, to_q),
+        (g2z, z, nz, z2_send, z2_recv, to_z),
+    )
+
+    def start(stage, x):
+        buf, mine, n, ssem, rsem, to = stage
+        sum_start(buf, mine, n, x, ssem, rsem, to)
+
+    def end(stage):
+        buf, mine, n, ssem, rsem, to = stage
+        return sum_end(buf, mine, n, ssem, rsem, to)
+
+    def first_factor():
+        pair = factor_pair(unpack(end(first[2]) * (1.0 / total_cols)))
+        pair_ref[...] = pair
+        vf_out[...] = transpose_left(pair)
+        for t in range(tp):
+            x = jnp.concatenate([jnp.zeros((width, TL), F32), own_tile(t)], axis=0)
+            v_out[:, t * TL : (t + 1) * TL] = jnp.dot(
+                pair, x, precision=HIGH, preferred_element_type=F32
+            )
+
     for k in range(nz + 2):
         if k < nz:
             arrive(k)
@@ -312,14 +361,14 @@
             relay(k - 1)
         if 2 <= k:
             finish(k - 2)
-
-    g = lax.fori_loop(
-        1, nr, lambda i, a: a + gz[i], gz[0]
-    )
-    g1[mc] = pack(fold(g))
-    for k in range(1, nc):
-        cc = (mc + k) % nc
-        send(g1.at[mc], g1.at[mc], g1_send.at[k - 1], g1_recv.at[mc], to_c(cc))
+        if k == 0:
+            start(first[0], gram_of(own_tile(t) for t in range(tp)))
+        elif k == 1:
+            start(first[1], end(first[0]))
+        elif k == 2:
+            start(first[2], end(first[1]))
+        elif k == max(3, nz - 1):
+            first_factor()
 
     def row_terms(r, _):
         x = prods[idx[r * each, 2]]
@@ -334,54 +383,23 @@
 
     for k in range(1, nc):
         cc = (mc + k) % nc
-        remote(g1.at[cc], g1.at[cc], g1_send.at[k - 1], g1_recv.at[cc], to_c(cc)).wait_recv()
-    gs = g1[0]
-    for cc in range(1, nc):
-        gs = gs + g1[cc]
-    pair = factor_pair(unpack(gs * (1.0 / total_cols)))
-    vf_out[...] = transpose_left(pair)
-    for t in range(tp):
-        x = jnp.concatenate(
-            [jnp.zeros((width, TL), F32), pt[z, gi, 0, t], pt[z, gi, 1, t]], axis=0
-        )
-        v_out[:, t * TL : (t + 1) * TL] = jnp.dot(
-            pair, x, precision=HIGH, preferred_element_type=F32
-        )
-
-    for k in range(1, nc):
-        cc = (mc + k) % nc
         remote(got_terms.at[cc], got_terms.at[cc], t_send.at[k - 1], t_recv.at[cc], to_c(cc)).wait_recv()
     root = math.sqrt(total_rows / total_cols)
 
-    acc = jnp.zeros((2 * width, 2 * width), F32)
+    pair = pair_ref[...]
     for i in range(rtc):
         r = mc * rtc + i
         x = terms[r]
         for k in range(1, nc):
             x = x + got_terms[(mc + k) % nc, i]
         uu = u[:, pl.ds(pl.multiple_of(r * TL, TL), TL)]
-        q = jnp.dot(
+        qt[i] = jnp.dot(
             pair, jnp.concatenate([-uu, root * x], axis=0), precision=HIGH, preferred_element_type=F32
         )
-        qt[i] = q
-        xx = jnp.concatenate(split(q), axis=0)
-        acc = acc + lax.dot_general(xx, xx, (((1,), (1,)), ((), ())), preferred_element_type=F32)
-
-    def sum_over(buf, mine, n, x, ssem, rsem, to):
-        buf[mine] = x
-        for k in range(1, n):
-            send(buf.at[mine], buf.at[mine], ssem.at[k - 1], rsem.at[mine], to((mine + k) % n))
-        for k in range(1, n):
-            o = (mine + k) % n
-            remote(buf.at[o], buf.at[o], ssem.at[k - 1], rsem.at[o], to(o)).wait_recv()
-        y = buf[0]
-        for o in range(1, n):
-            y = y + buf[o]
-        return y
-
-    x = sum_over(g2c, mc, nc, pack(fold(acc)), gc_send, gc_recv, to_c)
-    x = sum_over(g2q, gi, QUADS, x, gq_send, gq_recv, lambda q: {"row": base + q})
-    x = sum_over(g2z, z, nz, x, gg_send, gg_recv, to_z)
+    x = gram_of(qt[i] for i in range(rtc))
+    for stage in second:
+        start(stage, x)
+        x = end(stage)
     pair2 = factor_pair(unpack(x * (1.0 / total_rows)))
     uf_out[...] = transpose_left(pair2)
     for i in range(rtc):
@@ -391,6 +409,15 @@
         )
     for c in pending:
         c.wait_send()
+
+
+def hand_out(*refs):
+    src, dst, sem = refs[:4], refs[4:8], refs[8]
+    copies = [pltpu.make_async_copy(src[i], dst[i], sem.at[i]) for i in range(4)]
+    for c in copies:
+        c.start()
+    for c in copies:
+        c.wait()
 
 
 def per_device(tiles, tile_rows, tile_cols, exponents, u_basis, v_basis, prior):
@@ -412,7 +439,7 @@
     def sems(*shape):
         return [dma(shape), dma(shape)]
 
-    return pl.pallas_call(
+    outs = pl.pallas_call(
         functools.partial(kernel, nr, nc, block_rows * nr, block_cols * nc),
         out_shape=(
             jax.ShapeDtypeStruct((width, block_rows // nc), F32),
@@ -442,26 +469,27 @@
             pltpu.VMEM((ct, width, TL), F32),
             pltpu.VMEM((rt, width, TL), F32),
             pltpu.VMEM((nc, rtc, width, TL), F32),
-            pltpu.VMEM((nr, 2 * width, 2 * width), F32),
-            pltpu.VMEM((nc, half, 2 * width), F32),
-            pltpu.VMEM((nc, half, 2 * width), F32),
-            pltpu.VMEM((QUADS, half, 2 * width), F32),
-            pltpu.VMEM((nz, half, 2 * width), F32),
+            *[pltpu.VMEM((n, half, 2 * width), F32) for n in (nc, QUADS, nz)] * 2,
             pltpu.VMEM((rtc, width, TL), F32),
+            pltpu.VMEM((width, 2 * width), F32),
             *sems(nz, 6),
             dma((nz,)), dma((nz,)),
             dma((nz,)), dma((nz,)),
             *sems(nz, 6),
-            dma((nc,)), dma((nc,)),
-            dma((nc,)), dma((nc,)),
-            dma((nc,)), dma((nc,)),
-            dma((QUADS,)), dma((QUADS,)),
-            dma((nz,)), dma((nz,)),
+            *sems(nc),
+            *[x for n in (nc, QUADS, nz) for x in sems(n)] * 2,
         ],
         compiler_params=pltpu.CompilerParams(
             collective_id=0, has_side_effects=True, vmem_limit_bytes=56 * 1024 * 1024
         ),
     )(rows, cols, local, u_basis, expo, v_basis, prior)
+    return pl.pallas_call(
+        hand_out,
+        out_shape=tuple(jax.ShapeDtypeStruct(o.shape, o.dtype) for o in outs),
+        in_specs=[pl.BlockSpec(memory_space=pl.ANY)] * 4,
+        out_specs=(pl.BlockSpec(memory_space=pl.ANY),) * 4,
+        scratch_shapes=[dma((4,))],
+    )(*outs)
 
 
 def solution(mesh):

time: 77.3 us -> 85.7 us (1.11)
  Pallas kernels: 70.4 us -> 84.9 us
  local copies, waits for them, and re-layouts: 5.99 us -> 0 us
    pallas_call x0 -> x1, Pallas kernels: none -> 15 us  [per_device(): pl.pallas_call(hand_out, out_shape=tuple((jax.ShapeDtypeStruct(o.shape, o...]
    unnamed x4 -> x0, local copies, waits for them, and re-layouts: 5.99 us -> none
where the time goes in v3:
time: 85.7 us; the launch traced here: 85.6 us
  Pallas kernels  84.9 us (99%)
    pallas_call x1, Pallas kernels, per_device(): pl.pallas_call(functools.partial(kernel, nr, nc, block_rows * nr, block_c...  69.9 us
    pallas_call x1, Pallas kernels, per_device(): pl.pallas_call(hand_out, out_shape=tuple((jax.ShapeDtypeStruct(o.shape, o...  15 us

profile of v3, /device:TPU:0, one launch (start us, length us, event | category | flops | bytes accessed | tf_op | source)
XLA Modules:
  0.0 85.6 jit_solution(1635175934524033746)
XLA Ops:
  0.6 69.9 %shard_map.102 = (f32[64,1024]{1,0:T(8,128)}, f32[64,512]{1,0:T(8,128)}, f32[64,64]{1,0:T(8,128)}, f32[64,64]{1,0:T(8,128)}) custom-call(s32[1,64]{1,0:T(1,128)} %bitcast.6, s32[1,64]{1,0:T(1,128)} %bitcast.7, f32[64,128,128]{2,1,0:T(8,128)} %bitcast.4, f32[64,2048]{1,0:T(8,128)} %u_hbm.1, s32[64,1,128]{2,1,0:T(1,128)} %bitcast.5, f32[64,512]{1,0:T(8,128)} %v_hbm.1, ...), custom_call_target="tpu_custom_call" | custom-call | tf_op jit(solution)/shard_map/pallas_call | solution.py:442
  70.5 15.0 %shard_map.103 = (f32[64,1024]{1,0:T(8,128)}, f32[64,512]{1,0:T(8,128)}, f32[64,64]{1,0:T(8,128)}, f32[64,64]{1,0:T(8,128)}) custom-call(f32[64,1024]{1,0:T(8,128)} %get-tuple-element.8.refs_0_, f32[64,512]{1,0:T(8,128)} %get-tuple-element.9.refs_1_, f32[64,64]{1,0:T(8,128)} %get-tuple-element.10.refs_2_, f32[64,64]{1,0:T(8,128)} %get-tuple-element.11.refs_3_), custom_call_target="tpu_custom_call" | custom-call | tf_op jit(solution)/shard_map/pallas_call | solution.py:486

commit v4 on v3

--- a/solution.py
+++ b/solution.py
@@ -39,35 +39,50 @@
     return jnp.concatenate([jnp.where(lane < w, x, y), jnp.where(lane < w, y, x)], axis=0)
 
 
-def factor_pair(gram2, block=4):
-    w = gram2.shape[0]
-    row = lax.broadcasted_iota(jnp.int32, (w, 2 * w), 0)
-    lane = lax.broadcasted_iota(jnp.int32, (w, 2 * w), 1)
-    m = jnp.where(lane < w, gram2, jnp.where(lane - w == row, 1.0, 0.0).astype(F32))
-    done, top = [], 0
-    for j in range(0, w, block):
-        o = j - top
-        below = row[top:]
-        cols = [jnp.broadcast_to(m[:, j + i : j + i + 1], m.shape) for i in range(block)]
-        rows = [m[o + i : o + i + 1] for i in range(block)]
-        a = {(i, l): cols[l][o + i : o + i + 1] for i in range(block) for l in range(i, block)}
-        for i in range(block):
-            inv = 1.0 / a[i, i]
-            m = m - jnp.where(below > j + i, cols[i], 0.0) * (rows[i] * inv)
-            for l in range(i + 1, block):
-                s = a[i, l] * inv
-                rows[l] = rows[l] - s * rows[i]
-                cols[l] = cols[l] - s * cols[i]
-                for q in range(l, block):
-                    a[l, q] = a[l, q] - s * a[i, q]
-        if (j + block) % 8 == 0:
-            done.append(m[:8])
-            m = m[8:]
-            top += 8
-    m = jnp.concatenate(done, axis=0)
-    diag = jnp.sum(jnp.where(lane == row, m, 0.0), axis=1, keepdims=True)
-    m = m * (1.0 / jnp.sqrt(diag))
-    return jnp.where((lane >= w) | (lane >= row), m, 0.0)
+class Elimination:
+    def __init__(self, gram2):
+        w = gram2.shape[0]
+        self.row = lax.broadcasted_iota(jnp.int32, (w, 2 * w), 0)
+        self.lane = lax.broadcasted_iota(jnp.int32, (w, 2 * w), 1)
+        unit = jnp.where(self.lane - w == self.row, 1.0, 0.0).astype(F32)
+        self.m = jnp.where(self.lane < w, gram2, unit)
+        self.done, self.top, self.width = [], 0, w
+
+    def steps(self, begin, end, block=4):
+        m, top = self.m, self.top
+        for j in range(begin, end, block):
+            o = j - top
+            below = self.row[top:]
+            cols = [jnp.broadcast_to(m[:, j + i : j + i + 1], m.shape) for i in range(block)]
+            rows = [m[o + i : o + i + 1] for i in range(block)]
+            a = {(i, l): cols[l][o + i : o + i + 1] for i in range(block) for l in range(i, block)}
+            for i in range(block):
+                inv = 1.0 / a[i, i]
+                m = m - jnp.where(below > j + i, cols[i], 0.0) * (rows[i] * inv)
+                for l in range(i + 1, block):
+                    s = a[i, l] * inv
+                    rows[l] = rows[l] - s * rows[i]
+                    cols[l] = cols[l] - s * cols[i]
+                    for q in range(l, block):
+                        a[l, q] = a[l, q] - s * a[i, q]
+            if (j + block) % 8 == 0:
+                self.done.append(m[:8])
+                m = m[8:]
+                top += 8
+        self.m, self.top = m, top
+
+    def pair(self):
+        row, lane, w = self.row, self.lane, self.width
+        m = jnp.concatenate(self.done, axis=0)
+        diag = jnp.sum(jnp.where(lane == row, m, 0.0), axis=1, keepdims=True)
+        m = m * (1.0 / jnp.sqrt(diag))
+        return jnp.where((lane >= w) | (lane >= row), m, 0.0)
+
+
+def factor_pair(gram2):
+    e = Elimination(gram2)
+    e.steps(0, gram2.shape[0])
+    return e.pair()
 
 
 def transpose_left(pair):
@@ -249,9 +264,10 @@
                 x = x + gotz[(z + k) % nz, h, t]
             pt[z, gi, h, t] = x * sc - own[h * half : (h + 1) * half, t * TL : (t + 1) * TL]
 
-    for k in range(1, nz):
-        zs = (z + k) % nz
-        send(pt.at[z, gi], pt.at[z, gi], az_send.at[k - 1], az_recv.at[z], to_z(zs))
+    def spread(k):
+        if 1 <= k < nz:
+            zs = (z + k) % nz
+            send(pt.at[z, gi], pt.at[z, gi], az_send.at[k - 1], az_recv.at[z], to_z(zs))
 
     def ag(src, k, n, dev):
         send(src, src, ag_send.at[k, n], ag_recv.at[k, n], dev)
@@ -285,6 +301,7 @@
         zs = (z + nz - k) % nz
         if k:
             remote(pt.at[zs, gi], pt.at[zs, gi], az_send.at[0], az_recv.at[zs], to_z(zs)).wait_recv()
+        spread(k + 1)
         ag(pt.at[zs, gi, 0], k, 0, to_y)
         ag(pt.at[zs, gi, 1], k, 1, to_x)
         ag(pt.at[zs, gi, 0], k, 2, to_x)
@@ -344,8 +361,9 @@
         buf, mine, n, ssem, rsem, to = stage
         return sum_end(buf, mine, n, ssem, rsem, to)
 
-    def first_factor():
-        pair = factor_pair(unpack(end(first[2]) * (1.0 / total_cols)))
+    def first_factor(elim):
+        elim.steps(width // 2, width)
+        pair = elim.pair()
         pair_ref[...] = pair
         vf_out[...] = transpose_left(pair)
         for t in range(tp):
@@ -359,6 +377,8 @@
             arrive(k)
         if 1 <= k < nz + 1:
             relay(k - 1)
+        if k == max(4, nz):
+            first_factor(elim)
         if 2 <= k:
             finish(k - 2)
         if k == 0:
@@ -368,7 +388,8 @@
         elif k == 2:
             start(first[2], end(first[1]))
         elif k == max(3, nz - 1):
-            first_factor()
+            elim = Elimination(unpack(end(first[2]) * (1.0 / total_cols)))
+            elim.steps(0, width // 2)
 
     def row_terms(r, _):
         x = prods[idx[r * each, 2]]
@@ -412,12 +433,8 @@
 
 
 def hand_out(*refs):
-    src, dst, sem = refs[:4], refs[4:8], refs[8]
-    copies = [pltpu.make_async_copy(src[i], dst[i], sem.at[i]) for i in range(4)]
-    for c in copies:
-        c.start()
-    for c in copies:
-        c.wait()
+    for src, dst in zip(refs[:4], refs[4:]):
+        dst[...] = src[...]
 
 
 def per_device(tiles, tile_rows, tile_cols, exponents, u_basis, v_basis, prior):
@@ -486,9 +503,8 @@
     return pl.pallas_call(
         hand_out,
         out_shape=tuple(jax.ShapeDtypeStruct(o.shape, o.dtype) for o in outs),
-        in_specs=[pl.BlockSpec(memory_space=pl.ANY)] * 4,
-        out_specs=(pl.BlockSpec(memory_space=pl.ANY),) * 4,
-        scratch_shapes=[dma((4,))],
+        in_specs=[vm] * 4,
+        out_specs=(vm,) * 4,
     )(*outs)
 
 

time: 85.7 us -> 72.1 us (0.84)
  Pallas kernels: 84.9 us -> 71.3 us
    pallas_call x1, Pallas kernels: 15 us -> 1.79 us  [per_device(): pl.pallas_call(hand_out, out_shape=tuple((jax.ShapeDtypeStruct(o.shape, o...]
where the time goes in v4:
time: 72.1 us; the launch traced here: 71.9 us
  Pallas kernels  71.3 us (99%)
    pallas_call x1, Pallas kernels, per_device(): pl.pallas_call(functools.partial(kernel, nr, nc, block_rows * nr, block_c...  69.5 us
    pallas_call x1, Pallas kernels, per_device(): pl.pallas_call(hand_out, out_shape=tuple((jax.ShapeDtypeStruct(o.shape, o...  1.79 us

profile of v4, /device:TPU:0, one launch (start us, length us, event | category | flops | bytes accessed | tf_op | source)
XLA Modules:
  0.0 71.9 jit_solution(3625741813628108096)
XLA Ops:
  0.6 69.5 %shard_map.102 = (f32[64,1024]{1,0:T(8,128)}, f32[64,512]{1,0:T(8,128)}, f32[64,64]{1,0:T(8,128)}, f32[64,64]{1,0:T(8,128)}) custom-call(s32[1,64]{1,0:T(1,128)} %bitcast.6, s32[1,64]{1,0:T(1,128)} %bitcast.7, f32[64,128,128]{2,1,0:T(8,128)} %bitcast.4, f32[64,2048]{1,0:T(8,128)} %u_hbm.1, s32[64,1,128]{2,1,0:T(1,128)} %bitcast.5, f32[64,512]{1,0:T(8,128)} %v_hbm.1, ...), custom_call_target="tpu_custom_call" | custom-call | tf_op jit(solution)/shard_map/pallas_call | solution.py:459
  70.1 1.8 %shard_map.103 = (f32[64,1024]{1,0:T(8,128)}, f32[64,512]{1,0:T(8,128)}, f32[64,64]{1,0:T(8,128)}, f32[64,64]{1,0:T(8,128)}) custom-call(f32[64,1024]{1,0:T(8,128)} %get-tuple-element.8.refs_0_, f32[64,512]{1,0:T(8,128)} %get-tuple-element.9.refs_1_, f32[64,64]{1,0:T(8,128)} %get-tuple-element.10.refs_2_, f32[64,64]{1,0:T(8,128)} %get-tuple-element.11.refs_3_), custom_call_target="tpu_custom_call" | custom-call | tf_op jit(solution)/shard_map/pallas_call | solution.py:503

commit v5 on v4

--- a/solution.py
+++ b/solution.py
@@ -124,7 +124,8 @@
     half = width // 2
     rt = terms.shape[0]
     rtc = rt // nc
-    tp = part.shape[3]
+    ns, tps = part.shape[0], part.shape[4]
+    tp = ns * tps
     each = tiles.shape[0] // rt
     me = lax.axis_index("row")
     mc = lax.axis_index("col")
@@ -195,79 +196,85 @@
         y = x[:width] + x[width:]
         return y[:, :TL] + y[:, TL:]
 
-    def compute(k):
+    def column(st, zz, q, t):
+        return (zz * QUADS + q) * tp + st * tps + t
+
+    def compute(st, k):
         zz = (z + 1 + k) % nz
+        i = st * nz + k
         for n, q in enumerate((gd, gx, gy, gi)):
-            def body(t, _, q=q):
-                y = left_tile((zz * QUADS + q) * tp + t)
-                part[zz, q, 0, t] = y[:half]
-                part[zz, q, 1, t] = y[half:]
-                return 0
-            lax.fori_loop(0, tp, body, 0, unroll=True)
-            if n == 0 and k == 0:
+            for t in range(tps):
+                y = left_tile(column(st, zz, q, t))
+                part[st, zz, q, 0, t] = y[:half]
+                part[st, zz, q, 1, t] = y[half:]
+            if n == 0 and i == 0:
                 pl.semaphore_wait(barrier, len(peers))
             if n == 0:
-                send(part.at[zz, q, 0], got.at[k, 0], rs_send.at[k, 0], rs_recv.at[k, 0], to_x)
-                send(part.at[zz, q, 1], got.at[k, 1], rs_send.at[k, 1], rs_recv.at[k, 1], to_y)
+                rs(part.at[st, zz, q, 0], i, 0, to_x)
+                rs(part.at[st, zz, q, 1], i, 1, to_y)
             elif n == 1:
-                send(part.at[zz, q, 0], got.at[k, 2], rs_send.at[k, 2], rs_recv.at[k, 2], to_x)
+                rs(part.at[st, zz, q, 0], i, 2, to_x)
             elif n == 2:
-                send(part.at[zz, q, 1], got.at[k, 3], rs_send.at[k, 3], rs_recv.at[k, 3], to_y)
-
-    def rs_wait(k, n):
-        remote(got.at[k, n], got.at[k, n], rs_send.at[k, n], rs_recv.at[k, n], to_x).wait_recv()
-
-    def step2(k):
+                rs(part.at[st, zz, q, 1], i, 3, to_y)
+
+    def rs(src, i, n, dev):
+        send(src, got.at[i, n], rs_send.at[i, n], rs_recv.at[i, n], dev)
+
+    def rs_wait(i, n):
+        remote(got.at[i, n], got.at[i, n], rs_send.at[i, n], rs_recv.at[i, n], to_x).wait_recv()
+
+    def step2(st, k):
         zz = (z + 1 + k) % nz
-        rs_wait(k, 0)
-        part[zz, gy, 0] = part[zz, gy, 0] + got[k, 0]
-        send(part.at[zz, gy, 0], got.at[k, 4], rs_send.at[k, 4], rs_recv.at[k, 4], to_y)
-        rs_wait(k, 1)
-        part[zz, gx, 1] = part[zz, gx, 1] + got[k, 1]
-        send(part.at[zz, gx, 1], got.at[k, 5], rs_send.at[k, 5], rs_recv.at[k, 5], to_x)
-
-    def step3(k):
+        i = st * nz + k
+        rs_wait(i, 0)
+        part[st, zz, gy, 0] = part[st, zz, gy, 0] + got[i, 0]
+        rs(part.at[st, zz, gy, 0], i, 4, to_y)
+        rs_wait(i, 1)
+        part[st, zz, gx, 1] = part[st, zz, gx, 1] + got[i, 1]
+        rs(part.at[st, zz, gx, 1], i, 5, to_x)
+
+    def step3(st, k):
         zz = (z + 1 + k) % nz
+        i = st * nz + k
         for n in (2, 3, 4, 5):
-            rs_wait(k, n)
-        part[zz, gi, 0] = part[zz, gi, 0] + (got[k, 2] + got[k, 4])
-        part[zz, gi, 1] = part[zz, gi, 1] + (got[k, 3] + got[k, 5])
+            rs_wait(i, n)
+        part[st, zz, gi, 0] = part[st, zz, gi, 0] + (got[i, 2] + got[i, 4])
+        part[st, zz, gi, 1] = part[st, zz, gi, 1] + (got[i, 3] + got[i, 5])
         if k < nz - 1:
-            send(part.at[zz, gi], gotz.at[z], z_send.at[k], z_recv.at[z], to_z(zz))
-
-    for k in range(nz + 2):
-        if k < nz:
-            compute(k)
-        if k == 0:
-            tri = lax.broadcasted_iota(jnp.int32, prior.shape, 0) >= lax.broadcasted_iota(
-                jnp.int32, prior.shape, 1
-            )
-            low = jnp.where(tri, prior[...], 0.0)
-            own[...] = jnp.dot(low, v[...], precision=HIGH, preferred_element_type=F32)
-        if 1 <= k < nz + 1:
-            step2(k - 1)
-        if 2 <= k:
-            step3(k - 2)
+            send(part.at[st, zz, gi], gotz.at[st, z], z_send.at[st, k], z_recv.at[st, z], to_z(zz))
+
+    def own_term():
+        tri = lax.broadcasted_iota(jnp.int32, prior.shape, 0) >= lax.broadcasted_iota(
+            jnp.int32, prior.shape, 1
+        )
+        low = jnp.where(tri, prior[...], 0.0)
+        own[...] = jnp.dot(low, v[...], precision=HIGH, preferred_element_type=F32)
 
     def scale_of(j):
         e = expo[j]
-        return jnp.where(e % 2 == 1, 0.5, 1.0) * jnp.where(e >= 2, 0.25, 1.0)
-
-    for k in range(1, nz):
-        zs = (z + k) % nz
-        remote(gotz.at[zs], gotz.at[zs], z_send.at[k - 1], z_recv.at[zs], to_z(zs)).wait_recv()
-    for t in range(tp):
-        sc = scale_of(me * tp + t)
-        for h in range(2):
-            x = part[z, gi, h, t]
-            for k in range(1, nz):
-                x = x + gotz[(z + k) % nz, h, t]
-            pt[z, gi, h, t] = x * sc - own[h * half : (h + 1) * half, t * TL : (t + 1) * TL]
-
-    def spread(k):
+        return jnp.where((e & 1) == 1, 0.5, 1.0) * jnp.where(e >= 2, 0.25, 1.0)
+
+    def final(st):
+        for k in range(1, nz):
+            zs = (z + k) % nz
+            remote(
+                gotz.at[st, zs], gotz.at[st, zs], z_send.at[st, k - 1], z_recv.at[st, zs], to_z(zs)
+            ).wait_recv()
+        for t in range(tps):
+            at = (st * tps + t) * TL
+            sc = scale_of(column(st, z, gi, t))
+            for h in range(2):
+                x = part[st, z, gi, h, t]
+                for k in range(1, nz):
+                    x = x + gotz[st, (z + k) % nz, h, t]
+                pt[st, z, gi, h, t] = x * sc - own[h * half : (h + 1) * half, at : at + TL]
+
+    def spread(st, k):
         if 1 <= k < nz:
             zs = (z + k) % nz
-            send(pt.at[z, gi], pt.at[z, gi], az_send.at[k - 1], az_recv.at[z], to_z(zs))
+            send(
+                pt.at[st, z, gi], pt.at[st, z, gi], az_send.at[st, k - 1], az_recv.at[st, z], to_z(zs)
+            )
 
     def ag(src, k, n, dev):
         send(src, src, ag_send.at[k, n], ag_recv.at[k, n], dev)
@@ -275,10 +282,10 @@
     def ag_wait(dst, k, n):
         remote(dst, dst, ag_send.at[k, n], ag_recv.at[k, n], to_x).wait_recv()
 
-    def right_tiles(zz, q):
-        for t in range(tp):
-            j = (zz * QUADS + q) * tp + t
-            x = jnp.concatenate([pt[zz, q, 0, t], pt[zz, q, 1, t]], axis=0)
+    def right_tiles(st, zz, q):
+        for t in range(tps):
+            j = column(st, zz, q, t)
+            x = jnp.concatenate([pt[st, zz, q, 0, t], pt[st, zz, q, 1, t]], axis=0)
             xs = jnp.concatenate(split(x * scale_of(j)), axis=0)
             both = jnp.concatenate(split(tiles[idx[j, 0]]), axis=0)
             y = lax.dot_general(xs, both, (((1,), (1,)), ((), ())), preferred_element_type=F32)
@@ -295,35 +302,40 @@
         return pack(fold(acc))
 
     def own_tile(t):
-        return jnp.concatenate([pt[z, gi, 0, t], pt[z, gi, 1, t]], axis=0)
-
-    def arrive(k):
+        return jnp.concatenate([pt[t // tps, z, gi, h, t % tps] for h in range(2)], axis=0)
+
+    def arrive(st, k):
         zs = (z + nz - k) % nz
+        i = st * nz + k
         if k:
-            remote(pt.at[zs, gi], pt.at[zs, gi], az_send.at[0], az_recv.at[zs], to_z(zs)).wait_recv()
-        spread(k + 1)
-        ag(pt.at[zs, gi, 0], k, 0, to_y)
-        ag(pt.at[zs, gi, 1], k, 1, to_x)
-        ag(pt.at[zs, gi, 0], k, 2, to_x)
-        ag(pt.at[zs, gi, 1], k, 3, to_y)
-        right_tiles(zs, gi)
-
-    def relay(k):
+            remote(
+                pt.at[st, zs, gi], pt.at[st, zs, gi], az_send.at[st, 0], az_recv.at[st, zs], to_z(zs)
+            ).wait_recv()
+        spread(st, k + 1)
+        ag(pt.at[st, zs, gi, 0], i, 0, to_y)
+        ag(pt.at[st, zs, gi, 1], i, 1, to_x)
+        ag(pt.at[st, zs, gi, 0], i, 2, to_x)
+        ag(pt.at[st, zs, gi, 1], i, 3, to_y)
+        right_tiles(st, zs, gi)
+
+    def relay(st, k):
         zs = (z + nz - k) % nz
-        ag_wait(pt.at[zs, gy, 0], k, 0)
-        ag(pt.at[zs, gy, 0], k, 4, to_x)
-        ag_wait(pt.at[zs, gx, 1], k, 1)
-        ag(pt.at[zs, gx, 1], k, 5, to_y)
-
-    def finish(k):
+        i = st * nz + k
+        ag_wait(pt.at[st, zs, gy, 0], i, 0)
+        ag(pt.at[st, zs, gy, 0], i, 4, to_x)
+        ag_wait(pt.at[st, zs, gx, 1], i, 1)
+        ag(pt.at[st, zs, gx, 1], i, 5, to_y)
+
+    def finish(st, k):
         zs = (z + nz - k) % nz
-        ag_wait(pt.at[zs, gx, 0], k, 2)
-        right_tiles(zs, gx)
-        ag_wait(pt.at[zs, gy, 1], k, 3)
-        right_tiles(zs, gy)
-        ag_wait(pt.at[zs, gd, 0], k, 4)
-        ag_wait(pt.at[zs, gd, 1], k, 5)
-        right_tiles(zs, gd)
+        i = st * nz + k
+        ag_wait(pt.at[st, zs, gx, 0], i, 2)
+        right_tiles(st, zs, gx)
+        ag_wait(pt.at[st, zs, gy, 1], i, 3)
+        right_tiles(st, zs, gy)
+        ag_wait(pt.at[st, zs, gd, 0], i, 4)
+        ag_wait(pt.at[st, zs, gd, 1], i, 5)
+        right_tiles(st, zs, gd)
 
     def sum_start(buf, mine, n, x, ssem, rsem, to):
         buf[mine] = x
@@ -372,22 +384,39 @@
                 pair, x, precision=HIGH, preferred_element_type=F32
             )
 
-    for k in range(nz + 2):
-        if k < nz:
-            arrive(k)
-        if 1 <= k < nz + 1:
-            relay(k - 1)
-        if k == max(4, nz):
+    items = [(st, k) for st in range(ns) for k in range(nz)]
+    ends = [(st + 1) * nz + (1 if st == ns - 1 else 2) for st in range(ns)]
+    last = ends[-1]
+    third, fourth = last + max(3, nz - 1), last + max(4, nz)
+    for slot in range(last + nz + 2):
+        if slot < len(items):
+            compute(*items[slot])
+        if slot == 0:
+            own_term()
+        if 0 <= slot - 1 < len(items):
+            step2(*items[slot - 1])
+        if 0 <= slot - 2 < len(items):
+            step3(*items[slot - 2])
+        for st, begin in enumerate(ends):
+            if slot == begin:
+                final(st)
+            if 0 <= slot - begin < nz:
+                arrive(st, slot - begin)
+        for st, begin in enumerate(ends):
+            if 0 <= slot - begin - 1 < nz:
+                relay(st, slot - begin - 1)
+        if slot == fourth:
             first_factor(elim)
-        if 2 <= k:
-            finish(k - 2)
-        if k == 0:
+        for st, begin in enumerate(ends):
+            if 0 <= slot - begin - 2 < nz:
+                finish(st, slot - begin - 2)
+        if slot == last:
             start(first[0], gram_of(own_tile(t) for t in range(tp)))
-        elif k == 1:
+        elif slot == last + 1:
             start(first[1], end(first[0]))
-        elif k == 2:
+        elif slot == last + 2:
             start(first[2], end(first[1]))
-        elif k == max(3, nz - 1):
+        elif slot == third:
             elim = Elimination(unpack(end(first[2]) * (1.0 / total_cols)))
             elim.steps(0, width // 2)
 
@@ -397,11 +426,12 @@
             x = x + prods[idx[r * each + i, 2]]
         terms[r] = x
         return 0
-    lax.fori_loop(0, rt, row_terms, 0)
+
     for k in range(1, nc):
         cc = (mc + k) % nc
+        lax.fori_loop(cc * rtc, cc * rtc + rtc, row_terms, 0)
         send(terms.at[pl.ds(cc * rtc, rtc)], got_terms.at[mc], t_send.at[k - 1], t_recv.at[mc], to_c(cc))
-
+    lax.fori_loop(mc * rtc, mc * rtc + rtc, row_terms, 0)
     for k in range(1, nc):
         cc = (mc + k) % nc
         remote(got_terms.at[cc], got_terms.at[cc], t_send.at[k - 1], t_recv.at[cc], to_c(cc)).wait_recv()
@@ -447,6 +477,8 @@
     block_cols = exponents.shape[0]
     rt, ct = block_rows // TL, block_cols // TL
     tp = ct // nr
+    ns = 2 if tp % 2 == 0 else 1
+    tps = tp // ns
     rtc = rt // nc
     half = width // 2
     expo = exponents.reshape(ct, 1, TL)
@@ -478,21 +510,21 @@
             pltpu.SMEM((count, TL), jnp.int32),
             dma((8,)),
             pltpu.VMEM((rt, 2 * width, TL), BF16),
-            pltpu.VMEM((nz, QUADS, 2, tp, half, TL), F32),
-            pltpu.VMEM((nz, 6, tp, half, TL), F32),
-            pltpu.VMEM((nz, 2, tp, half, TL), F32),
+            pltpu.VMEM((ns, nz, QUADS, 2, tps, half, TL), F32),
+            pltpu.VMEM((ns * nz, 6, tps, half, TL), F32),
+            pltpu.VMEM((ns, nz, 2, tps, half, TL), F32),
             pltpu.VMEM((width, tp * TL), F32),
-            pltpu.VMEM((nz, QUADS, 2, tp, half, TL), F32),
+            pltpu.VMEM((ns, nz, QUADS, 2, tps, half, TL), F32),
             pltpu.VMEM((ct, width, TL), F32),
             pltpu.VMEM((rt, width, TL), F32),
             pltpu.VMEM((nc, rtc, width, TL), F32),
             *[pltpu.VMEM((n, half, 2 * width), F32) for n in (nc, QUADS, nz)] * 2,
             pltpu.VMEM((rtc, width, TL), F32),
             pltpu.VMEM((width, 2 * width), F32),
-            *sems(nz, 6),
-            dma((nz,)), dma((nz,)),
-            dma((nz,)), dma((nz,)),
-            *sems(nz, 6),
+            *sems(ns * nz, 6),
+            *sems(ns, nz),
+            *sems(ns, nz),
+            *sems(ns * nz, 6),
             *sems(nc),
             *[x for n in (nc, QUADS, nz) for x in sems(n)] * 2,
         ],

time: 72.1 us -> 73.8 us (1.024)
  Pallas kernels: 71.3 us -> 73 us
    pallas_call x1, Pallas kernels: 69.5 us -> 71.2 us  [per_device(): pl.pallas_call(functools.partial(kernel, nr, nc, block_rows * nr, block_c...]
where the time goes in v5:
time: 73.8 us; the launch traced here: 73.6 us
  Pallas kernels  73 us (99%)
    pallas_call x1, Pallas kernels, per_device(): pl.pallas_call(functools.partial(kernel, nr, nc, block_rows * nr, block_c...  71.2 us
    pallas_call x1, Pallas kernels, per_device(): pl.pallas_call(hand_out, out_shape=tuple((jax.ShapeDtypeStruct(o.shape, o...  1.79 us

profile of v5, /device:TPU:0, one launch (start us, length us, event | category | flops | bytes accessed | tf_op | source)
XLA Modules:
  0.0 73.6 jit_solution(3029413575335401714)
XLA Ops:
  0.6 71.2 %shard_map.102 = (f32[64,1024]{1,0:T(8,128)}, f32[64,512]{1,0:T(8,128)}, f32[64,64]{1,0:T(8,128)}, f32[64,64]{1,0:T(8,128)}) custom-call(s32[1,64]{1,0:T(1,128)} %bitcast.6, s32[1,64]{1,0:T(1,128)} %bitcast.7, f32[64,128,128]{2,1,0:T(8,128)} %bitcast.4, f32[64,2048]{1,0:T(8,128)} %u_hbm.1, s32[64,1,128]{2,1,0:T(1,128)} %bitcast.5, f32[64,512]{1,0:T(8,128)} %v_hbm.1, ...), custom_call_target="tpu_custom_call" | custom-call | tf_op jit(solution)/shard_map/pallas_call | solution.py:491
  71.8 1.8 %shard_map.103 = (f32[64,1024]{1,0:T(8,128)}, f32[64,512]{1,0:T(8,128)}, f32[64,64]{1,0:T(8,128)}, f32[64,64]{1,0:T(8,128)}) custom-call(f32[64,1024]{1,0:T(8,128)} %get-tuple-element.8.refs_0_, f32[64,512]{1,0:T(8,128)} %get-tuple-element.9.refs_1_, f32[64,64]{1,0:T(8,128)} %get-tuple-element.10.refs_2_, f32[64,64]{1,0:T(8,128)} %get-tuple-element.11.refs_3_), custom_call_target="tpu_custom_call" | custom-call | tf_op jit(solution)/shard_map/pallas_call | solution.py:535

commit v6 on v5

--- a/solution.py
+++ b/solution.py
@@ -24,6 +24,17 @@
     w = x.shape[0] // 2
     y = x[:w] + x[w:]
     return y + pltpu.roll(y, w, 1)
+
+
+def stacked(x):
+    return jnp.concatenate(split(x), axis=0)
+
+
+def times(left, x):
+    w = left.shape[0] // 2
+    y = jnp.dot(left, jnp.concatenate(split(x), axis=1), preferred_element_type=F32)
+    y = y[:w] + y[w:]
+    return y[:, :TL] + y[:, TL:]
 
 
 def pack(x):
@@ -158,10 +169,15 @@
         c.start()
         pending.append(c)
 
+    quarter = tiles.shape[0] // 4
     fetch = [
         pltpu.make_async_copy(src, dst, in_sem.at[i])
         for i, (src, dst) in enumerate((
-            (rows_hbm, rows_in), (cols_hbm, cols_in), (u_hbm, u), (tiles_hbm, tiles),
+            (rows_hbm, rows_in), (cols_hbm, cols_in), (u_hbm, u),
+            *[
+                (tiles_hbm.at[i : i + quarter], tiles.at[i : i + quarter])
+                for i in range(0, tiles.shape[0], quarter)
+            ],
             (expo_hbm, expo), (v_hbm, v), (prior_hbm, prior),
         ))
     ]
@@ -380,9 +396,7 @@
         vf_out[...] = transpose_left(pair)
         for t in range(tp):
             x = jnp.concatenate([jnp.zeros((width, TL), F32), own_tile(t)], axis=0)
-            v_out[:, t * TL : (t + 1) * TL] = jnp.dot(
-                pair, x, precision=HIGH, preferred_element_type=F32
-            )
+            v_out[:, t * TL : (t + 1) * TL] = times(stacked(pair), x)
 
     items = [(st, k) for st in range(ns) for k in range(nz)]
     ends = [(st + 1) * nz + (1 if st == ns - 1 else 2) for st in range(ns)]
@@ -420,44 +434,42 @@
             elim = Elimination(unpack(end(first[2]) * (1.0 / total_cols)))
             elim.steps(0, width // 2)
 
-    def row_terms(r, _):
+    def row_terms(r):
         x = prods[idx[r * each, 2]]
         for i in range(1, each):
             x = x + prods[idx[r * each + i, 2]]
         terms[r] = x
-        return 0
 
     for k in range(1, nc):
         cc = (mc + k) % nc
-        lax.fori_loop(cc * rtc, cc * rtc + rtc, row_terms, 0)
+        for i in range(rtc):
+            row_terms(cc * rtc + i)
         send(terms.at[pl.ds(cc * rtc, rtc)], got_terms.at[mc], t_send.at[k - 1], t_recv.at[mc], to_c(cc))
-    lax.fori_loop(mc * rtc, mc * rtc + rtc, row_terms, 0)
+    for i in range(rtc):
+        row_terms(mc * rtc + i)
     for k in range(1, nc):
         cc = (mc + k) % nc
         remote(got_terms.at[cc], got_terms.at[cc], t_send.at[k - 1], t_recv.at[cc], to_c(cc)).wait_recv()
     root = math.sqrt(total_rows / total_cols)
 
-    pair = pair_ref[...]
+    left = stacked(pair_ref[...])
     for i in range(rtc):
         r = mc * rtc + i
         x = terms[r]
         for k in range(1, nc):
             x = x + got_terms[(mc + k) % nc, i]
         uu = u[:, pl.ds(pl.multiple_of(r * TL, TL), TL)]
-        qt[i] = jnp.dot(
-            pair, jnp.concatenate([-uu, root * x], axis=0), precision=HIGH, preferred_element_type=F32
-        )
+        qt[i] = times(left, jnp.concatenate([-uu, root * x], axis=0))
     x = gram_of(qt[i] for i in range(rtc))
     for stage in second:
         start(stage, x)
         x = end(stage)
     pair2 = factor_pair(unpack(x * (1.0 / total_rows)))
+    left2 = stacked(pair2)
     uf_out[...] = transpose_left(pair2)
     for i in range(rtc):
         y = jnp.concatenate([jnp.zeros((width, TL), F32), qt[i]], axis=0)
-        u_out[:, i * TL : (i + 1) * TL] = jnp.dot(
-            pair2, y, precision=HIGH, preferred_element_type=F32
-        )
+        u_out[:, i * TL : (i + 1) * TL] = times(left2, y)
     for c in pending:
         c.wait_send()
 
@@ -477,7 +489,7 @@
     block_cols = exponents.shape[0]
     rt, ct = block_rows // TL, block_cols // TL
     tp = ct // nr
-    ns = 2 if tp % 2 == 0 else 1
+    ns = 1
     tps = tp // ns
     rtc = rt // nc
     half = width // 2
@@ -508,7 +520,7 @@
             pltpu.VMEM((width, width), F32),
             pltpu.VMEM((count, TL), jnp.int32),
             pltpu.SMEM((count, TL), jnp.int32),
-            dma((8,)),
+            dma((11,)),
             pltpu.VMEM((rt, 2 * width, TL), BF16),
             pltpu.VMEM((ns, nz, QUADS, 2, tps, half, TL), F32),
             pltpu.VMEM((ns * nz, 6, tps, half, TL), F32),

time: 73.8 us -> 71.4 us (0.967)
  Pallas kernels: 73 us -> 70.6 us
    pallas_call x1, Pallas kernels: 71.2 us -> 68.8 us  [per_device(): pl.pallas_call(functools.partial(kernel, nr, nc, block_rows * nr, block_c...]
where the time goes in v6:
time: 71.4 us; the launch traced here: 71.2 us
  Pallas kernels  70.6 us (99%)
    pallas_call x1, Pallas kernels, per_device(): pl.pallas_call(functools.partial(kernel, nr, nc, block_rows * nr, block_c...  68.8 us
    pallas_call x1, Pallas kernels, per_device(): pl.pallas_call(hand_out, out_shape=tuple((jax.ShapeDtypeStruct(o.shape, o...  1.79 us

profile of v6, /device:TPU:0, one launch (start us, length us, event | category | flops | bytes accessed | tf_op | source)
XLA Modules:
  0.0 71.2 jit_solution(3075362472324329115)
XLA Ops:
  0.6 68.8 %shard_map.102 = (f32[64,1024]{1,0:T(8,128)}, f32[64,512]{1,0:T(8,128)}, f32[64,64]{1,0:T(8,128)}, f32[64,64]{1,0:T(8,128)}) custom-call(s32[1,64]{1,0:T(1,128)} %bitcast.6, s32[1,64]{1,0:T(1,128)} %bitcast.7, f32[64,128,128]{2,1,0:T(8,128)} %bitcast.4, f32[64,2048]{1,0:T(8,128)} %u_hbm.1, s32[64,1,128]{2,1,0:T(1,128)} %bitcast.5, f32[64,512]{1,0:T(8,128)} %v_hbm.1, ...), custom_call_target="tpu_custom_call" | custom-call | tf_op jit(solution)/shard_map/pallas_call | solution.py:503
  69.4 1.8 %shard_map.103 = (f32[64,1024]{1,0:T(8,128)}, f32[64,512]{1,0:T(8,128)}, f32[64,64]{1,0:T(8,128)}, f32[64,64]{1,0:T(8,128)}) custom-call(f32[64,1024]{1,0:T(8,128)} %get-tuple-element.8.refs_0_, f32[64,512]{1,0:T(8,128)} %get-tuple-element.9.refs_1_, f32[64,64]{1,0:T(8,128)} %get-tuple-element.10.refs_2_, f32[64,64]{1,0:T(8,128)} %get-tuple-element.11.refs_3_), custom_call_target="tpu_custom_call" | custom-call | tf_op jit(solution)/shard_map/pallas_call | solution.py:547

commit v7 on v6

--- a/solution.py
+++ b/solution.py
@@ -150,6 +150,9 @@
     to_y = {"row": base + gy}
     to_d = {"row": base + gd}
 
+    near = sorted(range(nz), key=lambda o: min(o, nz - o))
+    far = near[::-1]
+
     def to_z(zz):
         return {"row": zz * QUADS + gi}
 
@@ -216,7 +219,7 @@
         return (zz * QUADS + q) * tp + st * tps + t
 
     def compute(st, k):
-        zz = (z + 1 + k) % nz
+        zz = (z + far[k]) % nz
         i = st * nz + k
         for n, q in enumerate((gd, gx, gy, gi)):
             for t in range(tps):
@@ -240,7 +243,7 @@
         remote(got.at[i, n], got.at[i, n], rs_send.at[i, n], rs_recv.at[i, n], to_x).wait_recv()
 
     def step2(st, k):
-        zz = (z + 1 + k) % nz
+        zz = (z + far[k]) % nz
         i = st * nz + k
         rs_wait(i, 0)
         part[st, zz, gy, 0] = part[st, zz, gy, 0] + got[i, 0]
@@ -250,7 +253,7 @@
         rs(part.at[st, zz, gx, 1], i, 5, to_x)
 
     def step3(st, k):
-        zz = (z + 1 + k) % nz
+        zz = (z + far[k]) % nz
         i = st * nz + k
         for n in (2, 3, 4, 5):
             rs_wait(i, n)
@@ -287,7 +290,7 @@
 
     def spread(st, k):
         if 1 <= k < nz:
-            zs = (z + k) % nz
+            zs = (z + near[k]) % nz
             send(
                 pt.at[st, z, gi], pt.at[st, z, gi], az_send.at[st, k - 1], az_recv.at[st, z], to_z(zs)
             )
@@ -321,13 +324,13 @@
         return jnp.concatenate([pt[t // tps, z, gi, h, t % tps] for h in range(2)], axis=0)
 
     def arrive(st, k):
-        zs = (z + nz - k) % nz
+        zs = (z + nz - near[k]) % nz
         i = st * nz + k
+        spread(st, k + 1)
         if k:
             remote(
                 pt.at[st, zs, gi], pt.at[st, zs, gi], az_send.at[st, 0], az_recv.at[st, zs], to_z(zs)
             ).wait_recv()
-        spread(st, k + 1)
         ag(pt.at[st, zs, gi, 0], i, 0, to_y)
         ag(pt.at[st, zs, gi, 1], i, 1, to_x)
         ag(pt.at[st, zs, gi, 0], i, 2, to_x)
@@ -335,7 +338,7 @@
         right_tiles(st, zs, gi)
 
     def relay(st, k):
-        zs = (z + nz - k) % nz
+        zs = (z + nz - near[k]) % nz
         i = st * nz + k
         ag_wait(pt.at[st, zs, gy, 0], i, 0)
         ag(pt.at[st, zs, gy, 0], i, 4, to_x)
@@ -343,7 +346,7 @@
         ag(pt.at[st, zs, gx, 1], i, 5, to_y)
 
     def finish(st, k):
-        zs = (z + nz - k) % nz
+        zs = (z + nz - near[k]) % nz
         i = st * nz + k
         ag_wait(pt.at[st, zs, gx, 0], i, 2)
         right_tiles(st, zs, gx)
@@ -412,13 +415,13 @@
         if 0 <= slot - 2 < len(items):
             step3(*items[slot - 2])
         for st, begin in enumerate(ends):
+            if 0 <= slot - begin - 1 < nz:
+                relay(st, slot - begin - 1)
+        for st, begin in enumerate(ends):
             if slot == begin:
                 final(st)
             if 0 <= slot - begin < nz:
                 arrive(st, slot - begin)
-        for st, begin in enumerate(ends):
-            if 0 <= slot - begin - 1 < nz:
-                relay(st, slot - begin - 1)
         if slot == fourth:
             first_factor(elim)
         for st, begin in enumerate(ends):

time: 71.4 us -> 69 us (0.966)
  Pallas kernels: 70.6 us -> 68.2 us
    pallas_call x1, Pallas kernels: 68.8 us -> 66.4 us  [per_device(): pl.pallas_call(functools.partial(kernel, nr, nc, block_rows * nr, block_c...]
where the time goes in v7:
time: 69 us; the launch traced here: 68.9 us
  Pallas kernels  68.2 us (99%)
    pallas_call x1, Pallas kernels, per_device(): pl.pallas_call(functools.partial(kernel, nr, nc, block_rows * nr, block_c...  66.4 us
    pallas_call x1, Pallas kernels, per_device(): pl.pallas_call(hand_out, out_shape=tuple((jax.ShapeDtypeStruct(o.shape, o...  1.79 us

profile of v7, /device:TPU:0, one launch (start us, length us, event | category | flops | bytes accessed | tf_op | source)
XLA Modules:
  0.0 68.9 jit_solution(8554477464874737512)
XLA Ops:
  0.6 66.4 %shard_map.102 = (f32[64,1024]{1,0:T(8,128)}, f32[64,512]{1,0:T(8,128)}, f32[64,64]{1,0:T(8,128)}, f32[64,64]{1,0:T(8,128)}) custom-call(s32[1,64]{1,0:T(1,128)} %bitcast.6, s32[1,64]{1,0:T(1,128)} %bitcast.7, f32[64,128,128]{2,1,0:T(8,128)} %bitcast.4, f32[64,2048]{1,0:T(8,128)} %u_hbm.1, s32[64,1,128]{2,1,0:T(1,128)} %bitcast.5, f32[64,512]{1,0:T(8,128)} %v_hbm.1, ...), custom_call_target="tpu_custom_call" | custom-call | tf_op jit(solution)/shard_map/pallas_call | solution.py:506
  67.1 1.8 %shard_map.103 = (f32[64,1024]{1,0:T(8,128)}, f32[64,512]{1,0:T(8,128)}, f32[64,64]{1,0:T(8,128)}, f32[64,64]{1,0:T(8,128)}) custom-call(f32[64,1024]{1,0:T(8,128)} %get-tuple-element.8.refs_0_, f32[64,512]{1,0:T(8,128)} %get-tuple-element.9.refs_1_, f32[64,64]{1,0:T(8,128)} %get-tuple-element.10.refs_2_, f32[64,64]{1,0:T(8,128)} %get-tuple-element.11.refs_3_), custom_call_target="tpu_custom_call" | custom-call | tf_op jit(solution)/shard_map/pallas_call | solution.py:550
